TPU v7x, 32 devices: a whole 2x2x4 slice. The times are simulated.
32 devices in a mesh: lat: 2 (over x), lon: 16 (over z, y, core).
Axes of the slice: x: 2, y: 2, z: 4, core: 2. Of those that a mesh axis runs over, the one named last changes fastest.
Arguments:
- field_state: bfloat16 [4, 16, 40960], P(None, 'lat', 'lon'), may hold values from -6 to 6
- reservoir_state: bfloat16 [4, 256, 4, 1024], P('lat', 'lon'), may hold values from -0.8984375 to 0.8984375
- coupling_blocks: bfloat16 [4, 2048, 128], P('lat'), may hold values from -0.375 to 0.375
- coupling_index: int32 [4, 8, 2], P('lat'), may hold values from 0 to 7, as said below
- input_blocks: bfloat16 [4, 1024, 128], P('lat'), may hold values from -0.5 to 0.5
- input_index: int32 [4, 8], P('lat'), may hold values from 0 to 19
- zonal_band_output_matrices: bfloat16 [2, 640, 1024], P('lat'), may hold values from -0.1875 to 0.1875
- region_band: int32 [4], P('lat'), may hold values from 0 to 1
Outputs:
- field_out: bfloat16 [4, 16, 40960], P(None, 'lat', 'lon')
- states_out: bfloat16 [4, 256, 4, 1024], P('lat', 'lon')
Inputs may be any that keep to these rules, and one draw needn't show every extreme that they name: `coupling_index`: the 2 block columns of one block-row differ. `region_band`: a band of the region row's own latitude group of 2 region rows.
All inputs are finite; a program needn't handle non-finite values.
Results may differ from a plain program's by a relative error of at most 0.0095.
Values may be sent and summed in bfloat16 or wider, within the bound.
No kernel may reach another device: no remote copies, remote signals or barrier semaphores. Data moves between devices by JAX's collectives and lax.ppermute only.
A program may use at most 64 MiB of HBM per device.

v0:
```python
import jax
import jax.numpy as jnp
from jax import lax
from jax.sharding import PartitionSpec as P

VARS = 40
STEPS = 3


def extended(cells, sides, width, closed):
    for axis, dim in sides:
        count = lax.axis_size(axis)
        ends = count if closed else count - 1
        head = lax.slice_in_dim(cells, 0, width, axis=dim)
        tail = lax.slice_in_dim(cells, cells.shape[dim] - width, cells.shape[dim], axis=dim)
        cells = jnp.concatenate(
            [
                lax.ppermute(tail, axis, [(i, (i + 1) % count) for i in range(ends)]),
                cells,
                lax.ppermute(head, axis, [((i + 1) % count, i) for i in range(ends)]),
            ],
            axis=dim,
        )
    return cells


def region_inputs(band_slab, region_count, vertical_quantity_total):
    perturbation_copies = band_slab.shape[0]
    pieces = band_slab.reshape(
        perturbation_copies, 8, region_count + 1, 4 * vertical_quantity_total
    )
    windows = jnp.concatenate([pieces[:, :, :-1], pieces[:, :, 1:]], axis=3)
    return windows.transpose(2, 0, 1, 3).reshape(
        region_count * perturbation_copies, 64 * vertical_quantity_total
    )


def reservoir_update(state_rows, input_rows, coupling, coupling_idx, driving, driving_idx):
    row_count = state_rows.shape[0]
    block_rows = coupling_idx.shape[0]
    slot_count = coupling_idx.shape[1]
    block_size = coupling.shape[-1]
    picked = jnp.take(state_rows.reshape(row_count, block_rows, block_size), coupling_idx, axis=1)
    blocks = coupling.reshape(block_rows, slot_count, block_size, block_size)
    recurrent = jnp.einsum("nbki,bkoi->nbo", picked, blocks, preferred_element_type=jnp.float32)
    chosen = jnp.take(input_rows.reshape(row_count, -1, block_size), driving_idx, axis=1)
    drive_blocks = driving.reshape(block_rows, block_size, block_size)
    drive_term = jnp.einsum(
        "nbi,boi->nbo", chosen, drive_blocks, preferred_element_type=jnp.float32
    )
    refreshed_activation = jnp.tanh(recurrent + drive_term)
    return refreshed_activation.reshape(row_count, block_rows * block_size).astype(jnp.bfloat16)


def per_device(
    field_state,
    reservoir_state,
    coupling_blocks,
    coupling_index,
    input_blocks,
    input_index,
    zonal_band_output_matrices,
    region_band,
):
    vertical_quantity_total = VARS
    perturbation_copies, lat_cells, flat_cols = field_state.shape
    meridional_sector_total = flat_cols // (4 * vertical_quantity_total)
    latitude_region_count = lat_cells // 4
    unit_count = reservoir_state.shape[-1]
    readout_local = zonal_band_output_matrices[0]
    current = field_state
    states_now = reservoir_state
    for step_index in range(STEPS):
        padded = extended(current, (("lat", 1),), 2, False)
        padded = extended(padded, (("lon", 2),), 2 * vertical_quantity_total, True)
        updated_rows = []
        for region_row in range(latitude_region_count):
            band_index = region_band[region_row]
            coupling = lax.dynamic_index_in_dim(coupling_blocks, band_index, 0, keepdims=False)
            coupling_idx = lax.dynamic_index_in_dim(coupling_index, band_index, 0, keepdims=False)
            driving = lax.dynamic_index_in_dim(input_blocks, band_index, 0, keepdims=False)
            driving_idx = lax.dynamic_index_in_dim(input_index, band_index, 0, keepdims=False)
            previous = states_now[region_row].reshape(
                meridional_sector_total * perturbation_copies, unit_count
            )
            inputs_now = region_inputs(
                padded[:, 4 * region_row : 4 * region_row + 8],
                meridional_sector_total,
                vertical_quantity_total,
            )
            updated_rows.append(
                reservoir_update(previous, inputs_now, coupling, coupling_idx, driving, driving_idx)
            )
        refreshed_activation = jnp.concatenate(updated_rows, axis=0)
        prediction_sequence = lax.dot_general(
            refreshed_activation,
            readout_local,
            (((1,), (1,)), ((), ())),
            preferred_element_type=jnp.float32,
        )
        prediction_sequence = prediction_sequence.astype(jnp.bfloat16)
        current = (
            prediction_sequence.reshape(
                latitude_region_count,
                meridional_sector_total,
                perturbation_copies,
                4,
                4 * vertical_quantity_total,
            )
            .transpose(2, 0, 3, 1, 4)
            .reshape(
                perturbation_copies,
                4 * latitude_region_count,
                meridional_sector_total * 4 * vertical_quantity_total,
            )
        )
        states_now = refreshed_activation.reshape(
            latitude_region_count, meridional_sector_total, perturbation_copies, unit_count
        )
    return (current, states_now)


def solution(mesh):
    return jax.shard_map(
        per_device,
        mesh=mesh,
        in_specs=(
            P(None, "lat", "lon"),
            P("lat", "lon", None, None),
            P("lat", None, None),
            P("lat", None, None),
            P("lat", None, None),
            P("lat", None),
            P("lat", None, None),
            P("lat"),
        ),
        out_specs=(P(None, "lat", "lon"), P("lat", "lon", None, None)),
        check_vma=False,
    )
```

profile of v0, /device:TPU:0, one launch (start us, length us, event | category | flops | bytes accessed | tf_op | source)
XLA Modules:
  0.0 122.5 jit_solution(6668732460257902703)
XLA Ops:
  0.6 1.8 %fusion.116 = (bf16[4,2,2560]{2,1,0:T(2,128)(2,1)}, bf16[4,2,2560]{2,1,0:T(2,128)(2,1)S(1)}) fusion(bf16[4,8,2560]{2,1,0:T(8,128)(2,1)} %param.12), kind=kLoop, calls=%fused_computation.171 | loop fusion | bytes 163840 | tf_op jit(solution)/shard_map/slice | solution.py:15
  2.4 4.8 %collective-permute-start = (bf16[4,2,2560]{2,1,0:T(2,128)(2,1)}, bf16[4,2,2560]{2,1,0:T(2,128)(2,1)S(1)}, u32[]{:S(2)}, u32[]{:S(2)}) collective-permute-start(bf16[4,2,2560]{2,1,0:T(2,128)(2,1)} %get-tuple-element.46), channel_id=1, source_target_pairs={{0,16},{1,17},{2,18},{3,19},{4,20},{5,21},{6,22},{7,23},{8,24},{9,... | collective-permute-start | bytes 122888 | tf_op jit(solution)/shard_map/ppermute | solution.py:18
  7.3 1.3 %collective-permute-start.1 = (bf16[4,2,2560]{2,1,0:T(2,128)(2,1)S(1)}, bf16[4,2,2560]{2,1,0:T(2,128)(2,1)}, u32[]{:S(2)}, u32[]{:S(2)}) collective-permute-start(bf16[4,2,2560]{2,1,0:T(2,128)(2,1)S(1)} %get-tuple-element.47), channel_id=1, source_target_pairs={{16,0},{17,1},{18,2},{19,3},{20,4},{21,5},{22,6},{23,7},{24,8},{25... | collective-permute-start | bytes 122888 | tf_op jit(solution)/shard_map/ppermute | solution.py:20
  8.6 1.3 %fusion.117 = (s32[1]{0:T(128)}, s32[1]{0:T(128)}) fusion(s32[2]{0:T(128)} %param.19), kind=kLoop, calls=%fused_computation.172 | loop fusion | bytes 16 | tf_op jit(solution)/shard_map/slice | solution.py:78
  13.5 1.4 %compare_and_fusion.1 = (pred[8]{0:T(512)(128)(4,1)}, s32[8]{0:T(128)S(1)}, pred[8]{0:T(512)(128)(4,1)}, s32[8]{0:T(128)S(1)}) fusion(s32[2,8]{1,0:T(2,128)} %param.17, s32[]{:T(128)S(6)} %select_n.47, s32[]{:T(128)S(6)} %select_n.46), kind=kLoop, calls=%fused_computation.135 | loop fusion | flops 96 | bytes 152 | tf_op jit(solution)/shard_map/jit(_take)/and | solution.py:46
  23.5 3.7 %collective-permute-start.3 = (bf16[4,12,80]{2,1,0:T(8,128)(2,1)S(1)}, bf16[4,12,80]{2,1,0:T(8,128)(2,1)S(1)}, u32[]{:S(2)}, u32[]{:S(2)}) collective-permute-start(bf16[4,12,80]{2,1,0:T(8,128)(2,1)S(1)} %get-tuple-element.38), channel_id=1, source_target_pairs={{1,0},{2,1},{3,2},{4,3},{5,4},{6,5},{7,6},{8,7},{9,8},{10,9},{11,1... | collective-permute-start | bytes 23048 | tf_op jit(solution)/shard_map/ppermute | solution.py:20
  27.3 1.4 %collective-permute-done.3 = bf16[4,12,80]{2,1,0:T(8,128)(2,1)S(1)} collective-permute-done((bf16[4,12,80]{2,1,0:T(8,128)(2,1)S(1)}, bf16[4,12,80]{2,1,0:T(8,128)(2,1)S(1)}, u32[]{:S(2)}, u32[]{:S(2)}) %collective-permute-start.3) | collective-permute-done | bytes 7712 | tf_op jit(solution)/shard_map/ppermute | solution.py:20
  28.7 4.4 %collective-permute-done.2 = bf16[4,12,80]{2,1,0:T(8,128)(2,1)S(1)} collective-permute-done((bf16[4,12,80]{2,1,0:T(8,128)(2,1)S(1)}, bf16[4,12,80]{2,1,0:T(8,128)(2,1)S(1)}, u32[]{:S(2)}, u32[]{:S(2)}) %collective-permute-start.2) | collective-permute-done | bytes 7712 | tf_op jit(solution)/shard_map/ppermute | solution.py:18
  34.2 1.8 %fusion.109 = (bf16[4,8,2720]{2,1,0:T(8,128)(2,1)}, bf16[4,8,2720]{2,1,0:T(8,128)(2,1)}) fusion(bf16[4,12,2720]{2,1,0:T(8,128)(2,1)} %concatenate.46), kind=kLoop, calls=%fused_computation.164 | loop fusion | bytes 696320 | tf_op jit(solution)/shard_map/slice | solution.py:87
  36.0 1.3 %reshape.104 = bf16[4,8,17,160]{3,2,1,0:T(8,128)(2,1)S(1)} reshape(bf16[4,8,2720]{2,1,0:T(8,128)(2,1)} %get-tuple-element.32) | data formatting | bytes 348160 | tf_op jit(solution)/shard_map/reshape | solution.py:29
  38.9 1.8 %copy.71 = bf16[64,20,128]{2,0,1:T(8,128)(2,1)} copy(bf16[64,20,128]{2,1,0:T(8,128)(2,1)} %reshape_reshape.19) | data formatting | bytes 655360 | tf_op jit(solution)/shard_map/reshape;reshape | solution.py:46
  40.7 1.3 %reshape.101 = bf16[4,8,17,160]{3,2,1,0:T(8,128)(2,1)S(1)} reshape(bf16[4,8,2720]{2,1,0:T(8,128)(2,1)} %get-tuple-element.33) | data formatting | bytes 348160 | tf_op jit(solution)/shard_map/reshape | solution.py:29
  43.6 1.8 %copy.64 = bf16[64,20,128]{2,0,1:T(8,128)(2,1)} copy(bf16[64,20,128]{2,1,0:T(8,128)(2,1)} %reshape_reshape.18) | data formatting | bytes 655360 | tf_op jit(solution)/shard_map/reshape;reshape | solution.py:46
  45.4 1.7 %gather_fusion.4 = bf16[8,64,128]{2,1,0:T(8,128)(2,1)S(1)} fusion(bf16[64,20,128]{2,0,1:T(8,128)(2,1)} %copy.71, s32[1024]{0:T(1024)} %get-tuple-element.54), kind=kCustom, calls=%fused_computation.7.clone | custom fusion | bytes 262176 | tf_op jit(solution)/shard_map/jit(_take)/gather | solution.py:46
  49.0 1.7 %gather_fusion.1 = bf16[8,64,128]{2,1,0:T(8,128)(2,1)S(1)} fusion(bf16[64,20,128]{2,0,1:T(8,128)(2,1)} %copy.64, s32[1024]{0:T(1024)} %get-tuple-element.56), kind=kCustom, calls=%fused_computation.1.clone | custom fusion | bytes 262176 | tf_op jit(solution)/shard_map/jit(_take)/gather | solution.py:46
  51.6 2.1 %fusion.12 = bf16[128,640]{1,0:T(8,128)(2,1)} fusion(bf16[1,640,1024]{2,1,0:T(8,128)(2,1)S(1)} %copy-done, bf16[64,1024]{1,0:T(8,128)(2,1)} %copy_bitcast_fusion.4, bf16[64,1024]{1,0:T(8,128)(2,1)S(1)} %copy_bitcast_fusion.5), kind=kOutput, calls=%fused_computation.36 | convolution fusion | flops 168378368 | bytes 1736704 | tf_op jit(solution)/shard_map/dot_general | solution.py:95
  55.7 1.3 %reshape.106 = bf16[4,8,2560]{2,1,0:T(8,128)(2,1)S(1)} reshape(bf16[4,2,4,16,160]{4,3,2,1,0:T(8,128)(2,1)} %bitcast.205) | data formatting | bytes 327680 | tf_op jit(solution)/shard_map/reshape | solution.py:111
  57.7 4.8 %collective-permute-start.4 = (bf16[4,2,2560]{2,1,0:T(2,128)(2,1)}, bf16[4,2,2560]{2,1,0:T(2,128)(2,1)S(1)}, u32[]{:S(2)}, u32[]{:S(2)}) collective-permute-start(bf16[4,2,2560]{2,1,0:T(2,128)(2,1)} %get-tuple-element.44), channel_id=1, source_target_pairs={{0,16},{1,17},{2,18},{3,19},{4,20},{5,21},{6,22},{7,23},{8,24},{9,... | collective-permute-start | bytes 122888 | tf_op jit(solution)/shard_map/ppermute | solution.py:18
  62.5 1.3 %collective-permute-start.5 = (bf16[4,2,2560]{2,1,0:T(2,128)(2,1)}, bf16[4,2,2560]{2,1,0:T(2,128)(2,1)}, u32[]{:S(2)}, u32[]{:S(2)}) collective-permute-start(bf16[4,2,2560]{2,1,0:T(2,128)(2,1)} %get-tuple-element.45), channel_id=1, source_target_pairs={{16,0},{17,1},{18,2},{19,3},{20,4},{21,5},{22,6},{23,7},{24,8},{25... | collective-permute-start | bytes 122888 | tf_op jit(solution)/shard_map/ppermute | solution.py:20
  66.0 2.6 %collective-permute-done.5 = bf16[4,2,2560]{2,1,0:T(2,128)(2,1)} collective-permute-done((bf16[4,2,2560]{2,1,0:T(2,128)(2,1)}, bf16[4,2,2560]{2,1,0:T(2,128)(2,1)}, u32[]{:S(2)}, u32[]{:S(2)}) %collective-permute-start.5) | collective-permute-done | bytes 40992 | tf_op jit(solution)/shard_map/ppermute | solution.py:20
  71.4 4.4 %collective-permute-done.6 = bf16[4,12,80]{2,1,0:T(8,128)(2,1)S(1)} collective-permute-done((bf16[4,12,80]{2,1,0:T(8,128)(2,1)S(1)}, bf16[4,12,80]{2,1,0:T(8,128)(2,1)S(1)}, u32[]{:S(2)}, u32[]{:S(2)}) %collective-permute-start.6) | collective-permute-done | bytes 7712 | tf_op jit(solution)/shard_map/ppermute | solution.py:18
  76.9 1.8 %fusion.108 = (bf16[4,8,2720]{2,1,0:T(8,128)(2,1)S(1)}, bf16[4,8,2720]{2,1,0:T(8,128)(2,1)}) fusion(bf16[4,12,2720]{2,1,0:T(8,128)(2,1)} %concatenate.51), kind=kLoop, calls=%fused_computation.163 | loop fusion | bytes 696320 | tf_op jit(solution)/shard_map/slice | solution.py:87
  81.7 1.3 %gather_fusion.8 = bf16[8,64,128]{2,1,0:T(8,128)(2,1)} fusion(bf16[64,20,128]{2,0,1:T(8,128)(2,1)S(1)} %copy.81, s32[1024]{0:T(1024)} %get-tuple-element.54), kind=kCustom, calls=%fused_computation.9.clone | custom fusion | bytes 262176 | tf_op jit(solution)/shard_map/jit(_take)/gather | solution.py:46
  85.5 1.3 %reshape.107 = bf16[4,8,17,160]{3,2,1,0:T(8,128)(2,1)S(1)} reshape(bf16[4,8,2720]{2,1,0:T(8,128)(2,1)} %get-tuple-element.31) | data formatting | bytes 348160 | tf_op jit(solution)/shard_map/reshape | solution.py:29
  89.5 1.3 %gather_fusion.5 = bf16[8,64,128]{2,1,0:T(8,128)(2,1)} fusion(bf16[64,20,128]{2,0,1:T(8,128)(2,1)S(1)} %copy.75, s32[1024]{0:T(1024)} %get-tuple-element.56), kind=kCustom, calls=%fused_computation.8.clone | custom fusion | bytes 262176 | tf_op jit(solution)/shard_map/jit(_take)/gather | solution.py:46
  90.9 1.3 %fusion.23 = bf16[8,128,64]{1,2,0:T(8,128)(2,1)S(1)} fusion(f32[8,128,64]{1,2,0:T(8,128)} %convolution_bitcast_fusion.4, bf16[8,128,128]{2,1,0:T(8,128)(2,1)S(1)} %bitcast.193, bf16[8,64,128]{2,1,0:T(8,128)(2,1)} %gather_fusion.5, pred[8]{0:T(512)(128)(4,1)S(1)} %copy-done.8), kind=kOutput, calls=%fused_computation.41 | convolution fusion | flops 16973824 | bytes 786440 | tf_op jit(solution)/shard_map/nbi,boi->nbo/dot_general | solution.py:48
  92.2 2.1 %fusion.15 = bf16[128,640]{1,0:T(8,128)(2,1)} fusion(bf16[1,640,1024]{2,1,0:T(8,128)(2,1)S(1)} %copy-done, bf16[64,1024]{1,0:T(8,128)(2,1)} %copy_bitcast_fusion.2, bf16[64,1024]{1,0:T(8,128)(2,1)S(1)} %copy_bitcast_fusion.3), kind=kOutput, calls=%fused_computation.37 | convolution fusion | flops 168378368 | bytes 1736704 | tf_op jit(solution)/shard_map/dot_general | solution.py:95
  96.3 1.3 %reshape.110 = bf16[4,8,2560]{2,1,0:T(8,128)(2,1)S(1)} reshape(bf16[4,2,4,16,160]{4,3,2,1,0:T(8,128)(2,1)} %bitcast.206) | data formatting | bytes 327680 | tf_op jit(solution)/shard_map/reshape | solution.py:111
  98.3 3.1 %collective-permute-start.8 = (bf16[4,2,2560]{2,1,0:T(2,128)(2,1)}, bf16[4,2,2560]{2,1,0:T(2,128)(2,1)}, u32[]{:S(2)}, u32[]{:S(2)}) collective-permute-start(bf16[4,2,2560]{2,1,0:T(2,128)(2,1)} %get-tuple-element.42), channel_id=1, source_target_pairs={{0,16},{1,17},{2,18},{3,19},{4,20},{5,21},{6,22},{7,23},{8,24},{9,... | collective-permute-start | bytes 122888 | tf_op jit(solution)/shard_map/ppermute | solution.py:18
  101.4 1.5 %collective-permute-start.9 = (bf16[4,2,2560]{2,1,0:T(2,128)(2,1)}, bf16[4,2,2560]{2,1,0:T(2,128)(2,1)}, u32[]{:S(2)}, u32[]{:S(2)}) collective-permute-start(bf16[4,2,2560]{2,1,0:T(2,128)(2,1)} %get-tuple-element.43), channel_id=1, source_target_pairs={{16,0},{17,1},{18,2},{19,3},{20,4},{21,5},{22,6},{23,7},{24,8},{25... | collective-permute-start | bytes 122888 | tf_op jit(solution)/shard_map/ppermute | solution.py:20
  104.5 3.1 %collective-permute-done.9 = bf16[4,2,2560]{2,1,0:T(2,128)(2,1)} collective-permute-done((bf16[4,2,2560]{2,1,0:T(2,128)(2,1)}, bf16[4,2,2560]{2,1,0:T(2,128)(2,1)}, u32[]{:S(2)}, u32[]{:S(2)}) %collective-permute-start.9) | collective-permute-done | bytes 40992 | tf_op jit(solution)/shard_map/ppermute | solution.py:20
  110.2 4.5 %collective-permute-done.10 = bf16[4,12,80]{2,1,0:T(8,128)(2,1)S(1)} collective-permute-done((bf16[4,12,80]{2,1,0:T(8,128)(2,1)S(1)}, bf16[4,12,80]{2,1,0:T(8,128)(2,1)S(1)}, u32[]{:S(2)}, u32[]{:S(2)}) %collective-permute-start.10) | collective-permute-done | bytes 7712 | tf_op jit(solution)/shard_map/ppermute | solution.py:18
  (122 shorter events, 47.2 us)
Async XLA Ops:
  0.6 51.0 %copy-start = (bf16[1,640,1024]{2,1,0:T(8,128)(2,1)S(1)}, bf16[1,640,1024]{2,1,0:T(8,128)(2,1)}, u32[]{:S(2)}) copy-start(bf16[1,640,1024]{2,1,0:T(8,128)(2,1)} %param.18) | copy-start | bytes 3932164
  2.4 20.0 %collective-permute-start = (bf16[4,2,2560]{2,1,0:T(2,128)(2,1)}, bf16[4,2,2560]{2,1,0:T(2,128)(2,1)S(1)}, u32[]{:S(2)}, u32[]{:S(2)}) collective-permute-start(bf16[4,2,2560]{2,1,0:T(2,128)(2,1)} %get-tuple-element.46), channel_id=1, source_target_pairs={{0,16},{1,17},{2,18},{3,19},{4,20},{5,21},{6,22},{7,23},{8,24},{9,... | collective-permute-start | bytes 122888 | tf_op jit(solution)/shard_map/ppermute | solution.py:18
  7.3 15.2 %collective-permute-start.1 = (bf16[4,2,2560]{2,1,0:T(2,128)(2,1)S(1)}, bf16[4,2,2560]{2,1,0:T(2,128)(2,1)}, u32[]{:S(2)}, u32[]{:S(2)}) collective-permute-start(bf16[4,2,2560]{2,1,0:T(2,128)(2,1)S(1)} %get-tuple-element.47), channel_id=1, source_target_pairs={{16,0},{17,1},{18,2},{19,3},{20,4},{21,5},{22,6},{23,7},{24,8},{25... | collective-permute-start | bytes 122888 | tf_op jit(solution)/shard_map/ppermute | solution.py:20
  21.0 1.4 %copy-start.6 = (bf16[4,8,2560]{2,1,0:T(8,128)(2,1)S(1)}, bf16[4,8,2560]{2,1,0:T(8,128)(2,1)}, u32[]{:S(2)}) copy-start(bf16[4,8,2560]{2,1,0:T(8,128)(2,1)} %param.12) | copy-start | bytes 491524
  21.1 6.2 %copy-start.5 = (bf16[2,1024,128]{2,1,0:T(8,128)(2,1)S(1)}, bf16[2,1024,128]{2,1,0:T(8,128)(2,1)}, u32[]{:S(2)}) copy-start(bf16[2,1024,128]{2,1,0:T(8,128)(2,1)} %param.16) | copy-start | bytes 1572868
  23.5 5.2 %collective-permute-start.3 = (bf16[4,12,80]{2,1,0:T(8,128)(2,1)S(1)}, bf16[4,12,80]{2,1,0:T(8,128)(2,1)S(1)}, u32[]{:S(2)}, u32[]{:S(2)}) collective-permute-start(bf16[4,12,80]{2,1,0:T(8,128)(2,1)S(1)} %get-tuple-element.38), channel_id=1, source_target_pairs={{1,0},{2,1},{3,2},{4,3},{5,4},{6,5},{7,6},{8,7},{9,8},{10,9},{11,1... | collective-permute-start | bytes 23048 | tf_op jit(solution)/shard_map/ppermute | solution.py:20
  27.2 5.9 %collective-permute-start.2 = (bf16[4,12,80]{2,1,0:T(8,128)(2,1)S(1)}, bf16[4,12,80]{2,1,0:T(8,128)(2,1)S(1)}, u32[]{:S(2)}, u32[]{:S(2)}) collective-permute-start(bf16[4,12,80]{2,1,0:T(8,128)(2,1)S(1)} %get-tuple-element.39), channel_id=1, source_target_pairs={{0,1},{1,2},{2,3},{3,4},{4,5},{5,6},{6,7},{7,8},{8,9},{9,10},{10,1... | collective-permute-start | bytes 23048 | tf_op jit(solution)/shard_map/ppermute | solution.py:18
  57.0 6.8 %copy-start.4 = (bf16[4,8,2560]{2,1,0:T(8,128)(2,1)}, bf16[4,8,2560]{2,1,0:T(8,128)(2,1)S(1)}, u32[]{:S(2)}) copy-start(bf16[4,8,2560]{2,1,0:T(8,128)(2,1)S(1)} %reshape.106) | copy-start | bytes 491524
  57.7 8.4 %collective-permute-start.4 = (bf16[4,2,2560]{2,1,0:T(2,128)(2,1)}, bf16[4,2,2560]{2,1,0:T(2,128)(2,1)S(1)}, u32[]{:S(2)}, u32[]{:S(2)}) collective-permute-start(bf16[4,2,2560]{2,1,0:T(2,128)(2,1)} %get-tuple-element.44), channel_id=1, source_target_pairs={{0,16},{1,17},{2,18},{3,19},{4,20},{5,21},{6,22},{7,23},{8,24},{9,... | collective-permute-start | bytes 122888 | tf_op jit(solution)/shard_map/ppermute | solution.py:18
  62.5 6.2 %collective-permute-start.5 = (bf16[4,2,2560]{2,1,0:T(2,128)(2,1)}, bf16[4,2,2560]{2,1,0:T(2,128)(2,1)}, u32[]{:S(2)}, u32[]{:S(2)}) collective-permute-start(bf16[4,2,2560]{2,1,0:T(2,128)(2,1)} %get-tuple-element.45), channel_id=1, source_target_pairs={{16,0},{17,1},{18,2},{19,3},{20,4},{21,5},{22,6},{23,7},{24,8},{25... | collective-permute-start | bytes 122888 | tf_op jit(solution)/shard_map/ppermute | solution.py:20
  69.9 1.6 %collective-permute-start.7 = (bf16[4,12,80]{2,1,0:T(8,128)(2,1)S(1)}, bf16[4,12,80]{2,1,0:T(8,128)(2,1)S(1)}, u32[]{:S(2)}, u32[]{:S(2)}) collective-permute-start(bf16[4,12,80]{2,1,0:T(8,128)(2,1)S(1)} %get-tuple-element.36), channel_id=1, source_target_pairs={{1,0},{2,1},{3,2},{4,3},{5,4},{6,5},{7,6},{8,7},{9,8},{10,9},{11,1... | collective-permute-start | bytes 23048 | tf_op jit(solution)/shard_map/ppermute | solution.py:20
  69.9 5.9 %collective-permute-start.6 = (bf16[4,12,80]{2,1,0:T(8,128)(2,1)S(1)}, bf16[4,12,80]{2,1,0:T(8,128)(2,1)S(1)}, u32[]{:S(2)}, u32[]{:S(2)}) collective-permute-start(bf16[4,12,80]{2,1,0:T(8,128)(2,1)S(1)} %get-tuple-element.37), channel_id=1, source_target_pairs={{0,1},{1,2},{2,3},{3,4},{4,5},{5,6},{6,7},{7,8},{8,9},{9,10},{10,1... | collective-permute-start | bytes 23048 | tf_op jit(solution)/shard_map/ppermute | solution.py:18
  79.3 3.8 %copy-start.2 = (f32[8,128,64]{1,2,0:T(8,128)S(1)}, f32[8,128,64]{1,2,0:T(8,128)}, u32[]{:S(2)}) copy-start(f32[8,128,64]{1,2,0:T(8,128)} %convolution_bitcast_fusion.1) | copy-start | bytes 786436
  87.1 3.8 %copy-start.8 = (pred[8]{0:T(512)(128)(4,1)S(1)}, pred[8]{0:T(512)(128)(4,1)}, u32[]{:S(2)}) copy-start(pred[8]{0:T(512)(128)(4,1)} %get-tuple-element.50) | copy-start | bytes 28
  97.6 6.3 %copy-start.3 = (bf16[4,8,2560]{2,1,0:T(8,128)(2,1)}, bf16[4,8,2560]{2,1,0:T(8,128)(2,1)S(1)}, u32[]{:S(2)}) copy-start(bf16[4,8,2560]{2,1,0:T(8,128)(2,1)S(1)} %reshape.110) | copy-start | bytes 491524
  98.3 6.2 %collective-permute-start.8 = (bf16[4,2,2560]{2,1,0:T(2,128)(2,1)}, bf16[4,2,2560]{2,1,0:T(2,128)(2,1)}, u32[]{:S(2)}, u32[]{:S(2)}) collective-permute-start(bf16[4,2,2560]{2,1,0:T(2,128)(2,1)} %get-tuple-element.42), channel_id=1, source_target_pairs={{0,16},{1,17},{2,18},{3,19},{4,20},{5,21},{6,22},{7,23},{8,24},{9,... | collective-permute-start | bytes 122888 | tf_op jit(solution)/shard_map/ppermute | solution.py:18
  101.4 6.2 %collective-permute-start.9 = (bf16[4,2,2560]{2,1,0:T(2,128)(2,1)}, bf16[4,2,2560]{2,1,0:T(2,128)(2,1)}, u32[]{:S(2)}, u32[]{:S(2)}) collective-permute-start(bf16[4,2,2560]{2,1,0:T(2,128)(2,1)} %get-tuple-element.43), channel_id=1, source_target_pairs={{16,0},{17,1},{18,2},{19,3},{20,4},{21,5},{22,6},{23,7},{24,8},{25... | collective-permute-start | bytes 122888 | tf_op jit(solution)/shard_map/ppermute | solution.py:20
  108.7 1.4 %collective-permute-start.11 = (bf16[4,12,80]{2,1,0:T(8,128)(2,1)S(1)}, bf16[4,12,80]{2,1,0:T(8,128)(2,1)S(1)}, u32[]{:S(2)}, u32[]{:S(2)}) collective-permute-start(bf16[4,12,80]{2,1,0:T(8,128)(2,1)S(1)} %get-tuple-element.34), channel_id=1, source_target_pairs={{1,0},{2,1},{3,2},{4,3},{5,4},{6,5},{7,6},{8,7},{9,8},{10,9},{11,1... | collective-permute-start | bytes 23048 | tf_op jit(solution)/shard_map/ppermute | solution.py:20
  108.7 5.9 %collective-permute-start.10 = (bf16[4,12,80]{2,1,0:T(8,128)(2,1)S(1)}, bf16[4,12,80]{2,1,0:T(8,128)(2,1)S(1)}, u32[]{:S(2)}, u32[]{:S(2)}) collective-permute-start(bf16[4,12,80]{2,1,0:T(8,128)(2,1)S(1)} %get-tuple-element.35), channel_id=1, source_target_pairs={{0,1},{1,2},{2,3},{3,4},{4,5},{5,6},{6,7},{7,8},{8,9},{9,10},{10,1... | collective-permute-start | bytes 23048 | tf_op jit(solution)/shard_map/ppermute | solution.py:18
  117.8 1.7 %copy-start.1 = (f32[8,128,64]{1,2,0:T(8,128)S(1)}, f32[8,128,64]{1,2,0:T(8,128)}, u32[]{:S(2)}) copy-start(f32[8,128,64]{1,2,0:T(8,128)} %convolution_bitcast_fusion) | copy-start | bytes 786436
  117.8 1.7 %copy-start.7 = (pred[8]{0:T(512)(128)(4,1)S(1)}, pred[8]{0:T(512)(128)(4,1)}, u32[]{:S(2)}) copy-start(pred[8]{0:T(512)(128)(4,1)} %get-tuple-element.4) | copy-start | bytes 28
where the time goes:
time: 124 us; the launch traced here: 123 us
  local copies, waits for them, and re-layouts  52.8 us (43%)
  starting transfers between devices  21.5 us (17%)
  waiting for transfers between devices  21 us (17%)
  matrix products  15.1 us (12%)
  other arithmetic  7.33 us (6%)
  between operations  4.85 us (4%)
    ppermute x6, starting transfers between devices, extended(): lax.ppermute(tail, axis, [(i, (i + 1) % count) for i in range(ends)])  13.7 us
    ppermute x6, waiting for transfers between devices, extended(): lax.ppermute(tail, axis, [(i, (i + 1) % count) for i in range(ends)])  13.3 us
    another operation x12, local copies, waits for them, and re-layouts, reservoir_update(): input_rows.reshape(row_count, -1, block_size)  11.8 us
    ppermute x6, starting transfers between devices, extended(): lax.ppermute(head, axis, [((i + 1) % count, i) for i in range(ends)])  7.77 us
    ppermute x6, waiting for transfers between devices, extended(): lax.ppermute(head, axis, [((i + 1) % count, i) for i in range(ends)])  7.7 us
    gather x6, local copies, waits for them, and re-layouts, reservoir_update(): jnp.take(input_rows.reshape(row_count, -1, block_size), driving_idx, axis=1)  7.41 us
    dot_general x6, matrix products, reservoir_update(): jnp.einsum('nbi,boi->nbo', chosen, drive_blocks, preferred_element_type=j...  5.44 us
    reshape x6, local copies, waits for them, and re-layouts, region_inputs(): band_slab.reshape(perturbation_copies, 8, region_count + 1, 4 * vertical_...  4.96 us
  transfers between devices with their start and end apart: 12, of which 7 were waited for; matrix products, arithmetic and copies ran while one was open for 13% of the time, Pallas kernels for 0%

commit v1 on v0

v1 whole, which is shorter than its diff:
```python
import functools

import jax
import jax.numpy as jnp
from jax import lax
from jax.experimental import pallas as pl
from jax.experimental.pallas import tpu as pltpu
from jax.sharding import PartitionSpec as P

VARS = 40
STEPS = 3
CELL = 4 * VARS
CHUNK = 4 * CELL
HALF = 512
NEAR = 256
MEM = 4
BLK = 128
BF = jnp.bfloat16
F32 = jnp.float32
VM = pl.BlockSpec(memory_space=pltpu.VMEM)
SM = pl.BlockSpec(memory_space=pltpu.SMEM)
HB = pl.BlockSpec(memory_space=pltpu.HBM)
NT = (((1,), (1,)), ((), ()))


def row_of(slot, row_ref):
    return row_ref[0] if slot == 0 else 1 - row_ref[0]


def message_kernel(parity_ref, field_hbm, state_hbm, first_ref, second_ref, field_ref, state_ref, sems):
    odd = parity_ref[0]
    lanes = field_hbm.shape[2] - HALF
    regions = state_hbm.shape[1]
    copies = []
    for k in range(2):
        low = odd if k == 0 else 1 - odd
        lane = pl.multiple_of((1 - low) * lanes, BLK)
        copies.append(pltpu.make_async_copy(field_hbm.at[:, :, pl.ds(lane, HALF)], field_ref.at[k], sems.at[k]))
        at = (1 - low) * (regions - 2)
        copies.append(pltpu.make_async_copy(state_hbm.at[:, pl.ds(at, 2)], state_ref.at[k], sems.at[2 + k]))
    for c in copies:
        c.start()
    for c in copies:
        c.wait()
    for k, out in enumerate((first_ref, second_ref)):
        for r in range(2):
            for j in range(2):
                out[r, j * MEM : (j + 1) * MEM] = state_ref[k, r, j]
        rows = jnp.transpose(field_ref[k].astype(F32), (1, 0, 2)).astype(BF)
        for d in range(8):
            at, lane = (d % 2) * MEM, (d // 2 % 2) * HALF
            out[2 + d // 4, at : at + MEM, lane : lane + HALF] = rows[d]


def setup_kernel(row_ref, band_ref, field_hbm, state_hbm, coup_hbm, inp_hbm, read_hbm, own_ref, s0_ref, s1_ref, w0_ref, w1_ref, read_ref, field_ref, state_ref, sems):
    copies = []

    def start(src, dst):
        copies.append(pltpu.make_async_copy(src, dst, sems.at[len(copies)]))
        copies[-1].start()

    start(field_hbm, field_ref)
    start(state_hbm, state_ref)
    for slot, w_ref in enumerate((w0_ref, w1_ref)):
        band = band_ref[row_of(slot, row_ref)]
        for k in range(2):
            start(coup_hbm.at[band, :, k], w_ref.at[:, :, k * BLK : (k + 1) * BLK])
        start(inp_hbm.at[band], w_ref.at[:, :, 2 * BLK :])
    start(read_hbm.at[0], read_ref)
    chunks = field_ref.shape[2] // CHUNK
    copies[0].wait()
    tiles = []
    for q in range(chunks):
        for m in range(MEM):
            tiles.append(field_ref[m, :, q * CHUNK : (q + 1) * CHUNK].astype(F32)[None])
    own_ref[...] = jnp.transpose(jnp.concatenate(tiles, axis=0), (1, 0, 2)).astype(BF)
    copies[1].wait()
    for slot, s_ref in enumerate((s0_ref, s1_ref)):
        r = row_of(slot, row_ref)
        rows = [state_ref[r, 4 * q + res].astype(F32) for res in range(4) for q in range(chunks)]
        s_ref[...] = jnp.concatenate(rows, axis=0).astype(BF)
    for c in copies[2:]:
        c.wait()


def pack(row, out_ref, k):
    last = row.shape[0] - MEM
    out_ref[k, :, :CHUNK] = row[MEM:last].astype(BF)
    half = NEAR // 2
    ends = [row[:MEM, CHUNK - NEAR : CHUNK - half], row[:MEM, CHUNK - half :], row[last:, :half], row[last:, half:NEAR]]
    out_ref[k, :, CHUNK:] = jnp.concatenate(ends, axis=0).astype(BF)


def unpack(msg):
    x = msg.astype(F32)
    own, ends = x[:, :CHUNK], x[:, CHUNK:]
    fill = jnp.zeros((MEM, CHUNK - 2 * ends.shape[1]), F32)
    before = jnp.concatenate([fill, ends[:MEM], ends[MEM : 2 * MEM]], axis=1)
    after = jnp.concatenate([ends[2 * MEM : 3 * MEM], ends[3 * MEM :], fill], axis=1)
    return jnp.concatenate([before, own, after], axis=0)


def sides(parity_ref, first, second):
    odd = parity_ref[0] == 1
    return jnp.where(odd, first, second), jnp.where(odd, second, first)


def first_edge_kernel(slots, parity_ref, row_ref, own_ref, first_ref, second_ref, *outs):
    for slot in range(slots):
        r = row_of(slot, row_ref)
        for k in range(2):
            at = k * MEM
            got = []
            for ref in (first_ref, second_ref):
                low = ref[2, at : at + MEM, :HALF].astype(F32)
                high = ref[3, at : at + MEM, HALF : 2 * HALF].astype(F32)
                got.append(jnp.where(r == 0, low, high))
            left, right = sides(parity_ref, *got)
            half = HALF // 2
            ends = [left[:, :half], left[:, half:], right[:, :half], right[:, half:]]
            outs[slot][k, :, :CHUNK] = own_ref[6 * r + k]
            outs[slot][k, :, CHUNK:] = jnp.concatenate(ends, axis=0).astype(BF)


def windows(lats, narrow):
    parts = [[] for _ in range(4)]
    for a in lats:
        rows = a.shape[0]
        before = jnp.concatenate([a[rows - MEM :, CHUNK - 2 * VARS :], a[: rows - MEM, CHUNK - 2 * VARS :]], axis=0)
        after = jnp.concatenate([a[MEM:, : 2 * VARS], a[:MEM, : 2 * VARS]], axis=0)
        ext = jnp.concatenate([before, a, after], axis=1)
        if narrow:
            ext = ext[MEM : rows - MEM]
        for res in range(4):
            parts[res].append(ext[:, CELL * res : CELL * res + 2 * CELL])
    return jnp.concatenate([jnp.concatenate(p, axis=1) for p in parts], axis=0).astype(BF)


def latitude(pred, d):
    per = pred.shape[0] // 4
    return jnp.concatenate([pred[res * per : (res + 1) * per, d * CELL : (d + 1) * CELL] for res in range(4)], axis=1)


def block_pre(b, band, s_ref, in_ref, cidx_ref, iidx_ref, w_ref):
    pieces = []
    for k in range(2):
        pieces.append(s_ref[:, pl.ds(pl.multiple_of(cidx_ref[band, k, b] * BLK, BLK), BLK)])
    pieces.append(in_ref[:, pl.ds(pl.multiple_of(iidx_ref[band, b] * BLK, BLK), BLK)])
    return lax.dot_general(jnp.concatenate(pieces, axis=1), w_ref[b], NT, preferred_element_type=F32)


def shadow_kernel(first, last, slots, row_ref, parity_ref, band_ref, cidx_ref, iidx_ref, w0_ref, w1_ref, read_ref, *rest):
    rest = list(rest)

    def take(n):
        got = rest[:n]
        del rest[:n]
        return got

    if first:
        own_ref, s0_ref, s1_ref, first_ref, second_ref = take(5)
    else:
        edge_refs, s_refs = take(slots), take(slots)
        far_refs = take(2 * (2 - slots))
    pre_refs = take(slots)
    out_far = take(2 * (2 - slots))
    xs_ref, in_ref, sc0_ref, sc1_ref, pre_ref = take(5)
    rows_at = [row_of(0, row_ref), row_of(1, row_ref)]
    w_refs = [w0_ref, w1_ref]

    for k in range(2):
        xs_ref[k] = jnp.zeros(xs_ref.shape[1:], F32)
        xs_ref[10 + k] = jnp.zeros(xs_ref.shape[1:], F32)
    if first:
        fill = jnp.zeros((MEM, CHUNK - HALF), F32)
        left, right = sides(parity_ref, first_ref[...].astype(F32), second_ref[...].astype(F32))
        for d in range(8):
            at, lane = (d % 2) * MEM, (d // 2 % 2) * HALF
            lo = jnp.concatenate([fill, left[2 + d // 4, at : at + MEM, lane : lane + HALF]], axis=1)
            hi = jnp.concatenate([right[2 + d // 4, at : at + MEM, lane : lane + HALF], fill], axis=1)
            xs_ref[2 + d] = jnp.concatenate([lo, own_ref[d].astype(F32), hi], axis=0)
        empty = jnp.zeros((MEM, s0_ref.shape[1]), F32)
        per = s0_ref.shape[0] // 4
        for slot, (src, dst) in enumerate(((s0_ref, sc0_ref), (s1_ref, sc1_ref))):
            low = rows_at[slot] == 0
            lo, hi = jnp.where(low, left[0], left[1]), jnp.where(low, right[0], right[1])
            rows = []
            for res in range(4):
                rows.append(lo[(res - 2) * MEM : (res - 1) * MEM] if res >= 2 else empty)
                rows.append(src[res * per : (res + 1) * per].astype(F32))
                rows.append(hi[res * MEM : (res + 1) * MEM] if res < 2 else empty)
            dst[...] = jnp.concatenate(rows, axis=0).astype(BF)
        s_refs = [sc0_ref, sc1_ref]
    else:
        for slot in range(slots):
            r = rows_at[slot]
            half = pl.multiple_of((1 - r) * 2 * CELL, 2 * CELL)
            pred = lax.dot_general(s_refs[slot][...], read_ref[pl.ds(half, 2 * CELL), :], NT, preferred_element_type=F32)
            for d in range(2):
                xs_ref[2 + 4 * r + 2 * r + d] = edge_refs[slot][d].astype(F32)
                xs_ref[2 + 4 * r + 2 * (1 - r) + d] = latitude(pred, d).astype(BF).astype(F32)
        if far_refs:
            for d in range(4):
                xs_ref[2 + 4 * rows_at[1] + d] = far_refs[0][d].astype(F32)
            s_refs = [s_refs[0], far_refs[1]]

    for slot in (1, 0):
        r = rows_at[slot]
        band = band_ref[r]
        in_ref[...] = windows([xs_ref[4 * r + d] for d in range(8)], False)
        blocks = iidx_ref.shape[1]
        pres = [block_pre(b, band, s_refs[slot], in_ref, cidx_ref, iidx_ref, w_refs[slot]) for b in range(blocks)]
        if slot < slots:
            if not last:
                for b in range(blocks):
                    pre_refs[slot][:, b * BLK : (b + 1) * BLK] = pres[b]
            else:
                for b in range(blocks):
                    pre_ref[:, b * BLK : (b + 1) * BLK] = pres[b]
                per = pre_ref.shape[0] // 4
                short = per - 2 * MEM
                for res in range(4):
                    pre_refs[slot][res * short : (res + 1) * short] = pre_ref[res * per + MEM : (res + 1) * per - MEM]
            continue
        state = jnp.concatenate([jnp.tanh(p).astype(BF) for p in pres], axis=1)
        pred = lax.dot_general(state, read_ref[...], NT, preferred_element_type=F32)
        if not last:
            for d in range(4):
                out_far[0][d] = latitude(pred, d).astype(BF)
            out_far[1][...] = state
            continue
        for d in range(4):
            out_far[0][d] = latitude(pred, d)[MEM:-MEM].astype(BF)
        stage_ref, sem = take(2)
        per = state.shape[0] // 4
        put_states(r, state, per, MEM, stage_ref, out_far[1], sem)


def put_states(r, state, per, skip, stage_ref, states_hbm, sem):
    for res in range(4):
        for q in range((per - 2 * skip) // MEM):
            at = res * per + skip + q * MEM
            stage_ref[4 * q + res] = state[at : at + MEM]
    copy = pltpu.make_async_copy(stage_ref, states_hbm.at[r], sem)
    copy.start()
    copy.wait()


def late_kernel(slot, last, final, row_ref, band_ref, iidx_ref, w_ref, read_ref, pre_ref, got_ref, *rest):
    r = row_of(slot, row_ref)
    band = band_ref[r]
    in_ref = rest[-1]
    in_ref[...] = windows([unpack(got_ref[k]) for k in range(2)], last)
    parts = []
    for b in range(iidx_ref.shape[1]):
        k = iidx_ref[band, b] - 15 * r
        used = jnp.logical_and(k >= 0, k < 5)
        at = pl.multiple_of(jnp.where(used, k, 0) * BLK, BLK)
        term = lax.dot_general(in_ref[:, pl.ds(at, BLK)], w_ref[b, :, 2 * BLK :], NT, preferred_element_type=F32)
        pre = pre_ref[:, b * BLK : (b + 1) * BLK] + jnp.where(used, term, 0.0)
        parts.append(jnp.tanh(pre).astype(BF))
    state = jnp.concatenate(parts, axis=1)
    if not last:
        msg_ref, edge_ref, s_ref = rest[:3]
        s_ref[...] = state
        half = pl.multiple_of(r * 2 * CELL, 2 * CELL)
        pred = lax.dot_general(state, read_ref[pl.ds(half, 2 * CELL), :], NT, preferred_element_type=F32)
        for d in range(2):
            row = latitude(pred, d)
            pack(row, msg_ref, d)
            edge_ref[d] = row.astype(BF)
        return
    pred = lax.dot_general(state, read_ref[...], NT, preferred_element_type=F32)
    mine = [latitude(pred, d) for d in range(4)]
    per = state.shape[0] // 4
    if not final:
        lats_ref, states_hbm, stage_ref, sem = rest[:4]
        for d in range(4):
            lats_ref[d] = mine[d].astype(BF)
        put_states(r, state, per, 0, stage_ref, states_hbm, sem)
        return
    other_ref, _, field_ref, states_hbm, stage_ref, sem = rest[:6]
    other = [other_ref[d].astype(F32) for d in range(4)]
    low = r == 0
    rows = [jnp.where(low, mine[d], other[d])[None] for d in range(4)]
    rows += [jnp.where(low, other[d], mine[d])[None] for d in range(4)]
    tiles = jnp.transpose(jnp.concatenate(rows, axis=0), (1, 0, 2)).astype(BF)
    for q in range(field_ref.shape[2] // CHUNK):
        for m in range(MEM):
            field_ref[m, :, q * CHUNK : (q + 1) * CHUNK] = tiles[q * MEM + m]
    put_states(r, state, per, 0, stage_ref, states_hbm, sem)


def call(kernel, out_shape, out_specs, scratch, operands, flops=0, aliases=None):
    arrays = [pltpu.with_memory_space_constraint(x, pltpu.HBM) if s is HB else x for x, s in operands]
    size = sum(x.size * x.dtype.itemsize for x, _ in operands)
    return pl.pallas_call(
        kernel,
        out_shape=out_shape,
        in_specs=[s for _, s in operands],
        out_specs=out_specs,
        scratch_shapes=scratch,
        input_output_aliases=aliases or {},
        compiler_params=pltpu.CompilerParams(vmem_limit_bytes=40 * 1024 * 1024),
        cost_estimate=pl.CostEstimate(flops=flops, bytes_accessed=size, transcendentals=0),
    )(*arrays)


def per_device(field_state, reservoir_state, coupling_blocks, coupling_index, input_blocks, input_index, readout, region_band):
    lat_count, lon_count = lax.axis_size("lat"), lax.axis_size("lon")
    lat_at = lax.axis_index("lat").astype(jnp.int32)
    lon_at = lax.axis_index("lon").astype(jnp.int32)
    region_rows, regions, members, units = reservoir_state.shape
    bands = coupling_blocks.shape[0]
    blocks = units // BLK
    outs = readout.shape[1]
    assert region_rows == 2 and members == MEM and regions % 4 == 0 and lon_count % 2 == 0
    chunks = regions // 4
    own_rows = chunks * MEM
    wide = own_rows + 2 * MEM
    rows = 4 * wide
    short = 4 * own_rows
    swap = lat_count == 2
    slots = 1 if swap else 2

    def bf(*dims):
        return jax.ShapeDtypeStruct(dims, BF)

    def vm(dims, dtype=BF):
        return pltpu.VMEM(dims, dtype)

    def trade(x, offset):
        pairs = []
        for j in range(lon_count):
            step = 1 if (j - offset) % 2 == 0 else -1
            pairs.append((j, (j + step) % lon_count))
        return lax.ppermute(x, "lon", pairs)

    def across(xs):
        if swap:
            return [lax.ppermute(xs[0], "lat", [(0, 1), (1, 0)])]
        up = lax.ppermute(xs[0], "lat", [(i + 1, i) for i in range(lat_count - 1)])
        down = lax.ppermute(xs[1], "lat", [(i, i + 1) for i in range(lat_count - 1)])
        return [down, up]

    row = ((1 - lat_at if swap else lat_at * 0).reshape(1), SM)
    parity = ((lon_at % 2).reshape(1), SM)
    band, cidx, iidx = (region_band, SM), (coupling_index.transpose(0, 2, 1), SM), (input_index, SM)
    flops = 2 * rows * units * (3 * BLK + outs)

    mail = call(
        message_kernel,
        [bf(4, 2 * MEM, 2 * HALF)] * 2,
        [VM] * 2,
        [vm((2, MEM, 8, HALF)), vm((2, region_rows, 2, MEM, units)), pltpu.SemaphoreType.DMA((4,))],
        [parity, (field_state, HB), (reservoir_state, HB)],
    )
    second = trade(mail[1], 1)
    first = trade(mail[0], 0)
    own, s0, s1, w0, w1, read = call(
        setup_kernel,
        [bf(8, own_rows, CHUNK), bf(short, units), bf(short, units), bf(blocks, BLK, 3 * BLK), bf(blocks, BLK, 3 * BLK), bf(outs, units)],
        [VM] * 6,
        [vm(field_state.shape), vm(reservoir_state.shape), pltpu.SemaphoreType.DMA((9,))],
        [
            row,
            band,
            (field_state, HB),
            (reservoir_state, HB),
            (coupling_blocks.reshape(bands, blocks, 2, BLK, BLK), HB),
            (input_blocks.reshape(bands, blocks, BLK, BLK), HB),
            (readout, HB),
        ],
        flops,
    )
    weights = [(w0, VM), (w1, VM), (read, VM)]
    sent = call(
        functools.partial(first_edge_kernel, slots),
        [bf(2, own_rows, CHUNK + HALF // 2)] * slots,
        [VM] * slots,
        [],
        [parity, row, (own, VM), (first, VM), (second, VM)],
    )
    source = [(x, VM) for x in (own, s0, s1, first, second)]
    states_shape = bf(region_rows, regions, MEM, units)
    stage = [vm((regions, MEM, units)), pltpu.SemaphoreType.DMA]

    for step in range(STEPS):
        last = step == STEPS - 1
        got = across(sent)
        pre_rows = short if last else rows
        out = [jax.ShapeDtypeStruct((pre_rows, units), F32)] * slots
        specs = [VM] * slots
        scratch = [vm((12, wide, CHUNK), F32), vm((rows, 16 * CELL)), vm((rows, units)), vm((rows, units)), vm((rows, units), F32)]
        if swap:
            out += [bf(4, own_rows if last else wide, CHUNK), states_shape if last else bf(rows, units)]
            specs += [VM, HB if last else VM]
            scratch += stage if last else []
        shadow = call(
            functools.partial(shadow_kernel, step == 0, last, slots),
            out,
            specs,
            scratch,
            [row, parity, band, cidx, iidx] + weights + source,
            2 * flops,
        )
        far = shadow[slots:]
        sent, edges, states = [None] * slots, [None] * slots, [None] * slots
        for slot in reversed(range(slots)):
            operands = [row, band, iidx, weights[slot], weights[2], (shadow[slot], VM), (got[slot], VM)]
            inputs = [vm((pre_rows, 4 * CELL))]
            if not last:
                sent[slot], edges[slot], states[slot] = call(
                    functools.partial(late_kernel, slot, False, False),
                    [bf(2, own_rows, CHUNK + NEAR // 2), bf(2, wide, CHUNK), bf(rows, units)],
                    [VM] * 3,
                    inputs,
                    operands,
                    flops,
                )
            elif slot == 1:
                far = call(
                    functools.partial(late_kernel, slot, True, False),
                    [bf(4, own_rows, CHUNK), states_shape],
                    [VM, HB],
                    stage + inputs,
                    operands,
                    flops,
                )
            else:
                return call(
                    functools.partial(late_kernel, slot, True, True),
                    [bf(MEM, 8, regions * CELL), states_shape],
                    [VM, HB],
                    stage + inputs,
                    operands + [(far[0], VM), (far[1], HB)],
                    flops,
                    {len(operands) + 1: 1},
                )
        source = [(x, VM) for x in edges + states + list(far)]


def solution(mesh):
    return jax.shard_map(
        per_device,
        mesh=mesh,
        in_specs=(
            P(None, "lat", "lon"),
            P("lat", "lon", None, None),
            P("lat", None, None),
            P("lat", None, None),
            P("lat", None, None),
            P("lat", None),
            P("lat", None, None),
            P("lat"),
        ),
        out_specs=(P(None, "lat", "lon"), P("lat", "lon", None, None)),
        check_vma=False,
    )
```

time: 124 us -> 29.8 us (0.24); the launches traced: 123 us -> 29.6 us
  local copies, waits for them, and re-layouts: 52.8 us -> 0.66 us
  waiting for transfers between devices: 21 us -> 0.64 us
  Pallas kernels: 0 us -> 16.7 us
  matrix products: 15.1 us -> 0 us
  starting transfers between devices: 21.5 us -> 10.9 us
  other arithmetic: 7.33 us -> 0 us
  between operations: 4.85 us -> 0.73 us
    ppermute x12 -> x5, waiting for transfers between devices: 21 us -> 0.64 us  [the longest x3 0.63 us: across(): return [lax.ppermute(xs[0], 'lat', [(0, 1), (1, 0)])]]
    pallas_call x0 -> x9, Pallas kernels: none -> 16.7 us  [call(): pl.pallas_call(kernel, out_shape=out_shape, in_specs=[s for _, s in opera...]
    dot_general x15 -> x0, matrix products: 15.1 us -> none  [the longest x6 5.44 us: reservoir_update(): jnp.einsum('nbi,boi->nbo', chosen, drive_blocks, preferred_element_type=j...]
    reshape x15 -> x0, local copies, waits for them, and re-layouts: 13.4 us -> none  [the longest x6 4.96 us: region_inputs(): band_slab.reshape(perturbation_copies, 8, region_count + 1, 4 * vertical_...]
    another operation x16 -> x0, local copies, waits for them, and re-layouts: 12 us -> none  [the longest x12 11.8 us: reservoir_update(): input_rows.reshape(row_count, -1, block_size)]
    gather x12 -> x0, local copies, waits for them, and re-layouts: 11 us -> none  [the longest x6 7.41 us: reservoir_update(): jnp.take(input_rows.reshape(row_count, -1, block_size), driving_idx, axis=1)]
    ppermute x12 -> x5, starting transfers between devices: 21.5 us -> 10.9 us  [the longest x2 6.18 us: trade(): return lax.ppermute(x, 'lon', pairs)]
    slice x17 -> x0, local copies, waits for them, and re-layouts: 10.1 us -> none  [the longest x3 3.62 us: per_device(): padded[:, 4 * region_row:4 * region_row + 8]]
  transfers between devices with their start and end apart: 12 -> 5, of which waited for: 7 -> 2; matrix products, arithmetic and copies ran while one was open for 13% -> 0% of each run, Pallas kernels for 0% -> 36%
where the time goes in v1:
time: 29.8 us; the launch traced here: 29.6 us
  Pallas kernels  16.7 us (56%)
  starting transfers between devices  10.9 us (37%)
  between operations  0.73 us (2%)
  local copies, waits for them, and re-layouts  0.66 us (2%)
  waiting for transfers between devices  0.64 us (2%)
    pallas_call x9, Pallas kernels, call(): pl.pallas_call(kernel, out_shape=out_shape, in_specs=[s for _, s in opera...  16.7 us
    ppermute x2, starting transfers between devices, trade(): return lax.ppermute(x, 'lon', pairs)  6.18 us
    ppermute x3, starting transfers between devices, across(): return [lax.ppermute(xs[0], 'lat', [(0, 1), (1, 0)])]  4.69 us
    unnamed x6, local copies, waits for them, and re-layouts  0.66 us
    ppermute x3, waiting for transfers between devices, across(): return [lax.ppermute(xs[0], 'lat', [(0, 1), (1, 0)])]  0.63 us
  transfers between devices with their start and end apart: 5, of which 2 were waited for; matrix products, arithmetic and copies ran while one was open for 0% of the time, Pallas kernels for 36%

profile of v1, /device:TPU:0, one launch (start us, length us, event | category | flops | bytes accessed | tf_op | source)
XLA Modules:
  0.0 29.6 jit_solution(17982628618029903944)
XLA Ops:
  0.6 0.9 %shard_map.96 = (bf16[4,8,1024]{2,1,0:T(8,128)(2,1)S(1)}, bf16[4,8,1024]{2,1,0:T(8,128)(2,1)S(1)}) custom-call(s32[1]{0:T(128)} %bitcast.3.parity_ref, bf16[4,8,2560]{2,1,0:T(8,128)(2,1)} %field_hbm.3, bf16[2,16,4,1024]{3,2,1,0:T(4,128)(2,1)} %state_hbm.3), custom_call_target="tpu_custom_call" | custom-call | bytes 425988 | tf_op jit(solution)/shard_map/pallas_call | solution.py:297
  1.5 0.5 %collective-permute-start = (bf16[4,8,1024]{2,1,0:T(8,128)(2,1)S(1)}, bf16[4,8,1024]{2,1,0:T(8,128)(2,1)S(1)}, u32[]{:S(2)}, u32[]{:S(2)}) collective-permute-start(bf16[4,8,1024]{2,1,0:T(8,128)(2,1)S(1)} %get-tuple-element.31), channel_id=1, source_target_pairs={{0,1},{1,0},{2,3},{3,2},{4,5},{5,4},{6,7},{7,6},{8,9},{9,8},{10,11... | collective-permute-start | bytes 196616 | tf_op jit(solution)/shard_map/ppermute | solution.py:337
  2.1 5.7 %collective-permute-start.1 = (bf16[4,8,1024]{2,1,0:T(8,128)(2,1)S(1)}, bf16[4,8,1024]{2,1,0:T(8,128)(2,1)S(1)}, u32[]{:S(2)}, u32[]{:S(2)}) collective-permute-start(bf16[4,8,1024]{2,1,0:T(8,128)(2,1)S(1)} %get-tuple-element.32), channel_id=1, source_target_pairs={{0,15},{1,2},{2,1},{3,4},{4,3},{5,6},{6,5},{7,8},{8,7},{9,10},{10,... | collective-permute-start | bytes 196616 | tf_op jit(solution)/shard_map/ppermute | solution.py:337
  7.7 0.0 copy-start.1
  7.7 0.7 %copy-done.1 = s32[2]{0:T(128)S(1)} copy-done((s32[2]{0:T(128)S(1)}, s32[2]{0:T(128)}, u32[]{:S(2)}) %copy-start.1) | copy-done | bytes 32
  8.4 0.0 copy-start
  8.4 0.0 copy-start.2
  8.4 2.6 %shard_map.95 = (bf16[8,16,640]{2,1,0:T(8,128)(2,1)S(1)}, bf16[64,1024]{1,0:T(8,128)(2,1)S(1)}, bf16[64,1024]{1,0:T(8,128)(2,1)S(1)}, bf16[8,128,384]{2,1,0:T(8,...) custom-call(s32[1]{0:T(128)} %bitcast.row_ref, s32[2]{0:T(128)S(1)} %copy-done.1, ...), custom_call_target="tpu_custom_call" | custom-call | flops 201326592 | bytes 3309580 | tf_op jit(solution)/shard_map/pallas_call | solution.py:297
  11.0 0.0 collective-permute-done.rest_3_.first_ref
  11.0 0.0 collective-permute-done.1.rest_4_.second_ref
  11.0 1.6 %collective-permute-start.2 = (bf16[2,16,896]{2,1,0:T(8,128)(2,1)S(1)}, bf16[2,16,896]{2,1,0:T(8,128)(2,1)S(1)}, u32[]{:S(2)}, u32[]{:S(2)}) collective-permute-start(bf16[2,16,896]{2,1,0:T(8,128)(2,1)S(1)} %shard_map.98), channel_id=1, source_target_pairs={{0,16},{16,0},{1,17},{17,1},{2,18},{18,2},{3,19},{19,3},{4,20},{20... | collective-permute-start | bytes 172040 | tf_op jit(solution)/shard_map/ppermute | solution.py:341
  12.6 0.0 copy-done
  12.6 0.0 copy-done.2
  12.6 2.2 %shard_map.97 = (f32[96,1024]{1,0:T(8,128)S(1)}, bf16[4,24,640]{2,1,0:T(8,128)(2,1)S(1)}, bf16[96,1024]{1,0:T(8,128)(2,1)S(1)}) custom-call(s32[1]{0:T(128)} %bitcast.row_ref, s32[1]{0:T(128)} %bitcast.3.parity_ref, s32[2]{0:T(128)S(1)} %copy-done.1, s32[2,2,8]{2,1,0:T(2,128)S(1)} %bitcast.5, s32[2,8]{1,0:T(2,128)S(1)} %copy-done, ...), custom_call_target="tpu_custom_call" | custom-call | flops 402653184 | bytes 3440848 | tf_op jit(solution)/shard_map/pallas_call | solution.py:297
  14.7 0.5 %collective-permute-done.2.got_ref = bf16[2,16,896]{2,1,0:T(8,128)(2,1)S(1)} collective-permute-done((bf16[2,16,896]{2,1,0:T(8,128)(2,1)S(1)}, bf16[2,16,896]{2,1,0:T(8,128)(2,1)S(1)}, u32[]{:S(2)}, u32[]{:S(2)}) %collective-permute-start.2) | collective-permute-done | bytes 57376 | tf_op jit(solution)/shard_map/ppermute | solution.py:341
  15.3 1.3 %shard_map.99 = (bf16[2,16,768]{2,1,0:T(8,128)(2,1)S(1)}, bf16[2,24,640]{2,1,0:T(8,128)(2,1)S(1)}, bf16[96,1024]{1,0:T(8,128)(2,1)S(1)}) custom-call(s32[1]{0:T(128)} %bitcast.row_ref, s32[2]{0:T(128)S(1)} %copy-done.1, s32[2,8]{1,0:T(2,128)S(1)} %copy-done, bf16[8,128,384]{2,1,0:T(8,128)(2,1)S(1)} %get-tuple-element.25.w0_ref.w_ref, ...), custom_call_target="tpu_custom_call" | custom-call | flops 201326592 | bytes 2547788 | tf_op jit(solution)/shard_map/pallas_call | solution.py:297
  16.6 1.7 %collective-permute-start.3 = (bf16[2,16,768]{2,1,0:T(8,128)(2,1)S(1)}, bf16[2,16,768]{2,1,0:T(8,128)(2,1)S(1)}, u32[]{:S(2)}, u32[]{:S(2)}) collective-permute-start(bf16[2,16,768]{2,1,0:T(8,128)(2,1)S(1)} %get-tuple-element.39), channel_id=1, source_target_pairs={{0,16},{16,0},{1,17},{17,1},{2,18},{18,2},{3,19},{19,3},{4,20},{20... | collective-permute-start | bytes 147464 | tf_op jit(solution)/shard_map/ppermute | solution.py:341
  18.3 2.6 %shard_map.100 = (f32[96,1024]{1,0:T(8,128)S(1)}, bf16[4,24,640]{2,1,0:T(8,128)(2,1)S(1)}, bf16[96,1024]{1,0:T(8,128)(2,1)S(1)}) custom-call(s32[1]{0:T(128)} %bitcast.row_ref, s32[1]{0:T(128)} %bitcast.3.parity_ref, s32[2]{0:T(128)S(1)} %copy-done.1, s32[2,2,8]{2,1,0:T(2,128)S(1)} %bitcast.6, s32[2,8]{1,0:T(2,128)S(1)} %copy-done, ...), custom_call_target="tpu_custom_call" | custom-call | flops 402653184 | bytes 3461328 | tf_op jit(solution)/shard_map/pallas_call | solution.py:297
  21.0 0.1 collective-permute-done.3.got_ref
  21.1 1.3 %shard_map.101 = (bf16[2,16,768]{2,1,0:T(8,128)(2,1)S(1)}, bf16[2,24,640]{2,1,0:T(8,128)(2,1)S(1)}, bf16[96,1024]{1,0:T(8,128)(2,1)S(1)}) custom-call(s32[1]{0:T(128)} %bitcast.row_ref, s32[2]{0:T(128)S(1)} %copy-done.1, s32[2,8]{1,0:T(2,128)S(1)} %copy-done, bf16[8,128,384]{2,1,0:T(8,128)(2,1)S(1)} %get-tuple-element.25.w0_ref.w_ref, ...), custom_call_target="tpu_custom_call" | custom-call | flops 201326592 | bytes 2539596 | tf_op jit(solution)/shard_map/pallas_call | solution.py:297
  22.4 1.4 %collective-permute-start.4 = (bf16[2,16,768]{2,1,0:T(8,128)(2,1)S(1)}, bf16[2,16,768]{2,1,0:T(8,128)(2,1)S(1)}, u32[]{:S(2)}, u32[]{:S(2)}) collective-permute-start(bf16[2,16,768]{2,1,0:T(8,128)(2,1)S(1)} %get-tuple-element.45), channel_id=1, source_target_pairs={{0,16},{16,0},{1,17},{17,1},{2,18},{18,2},{3,19},{19,3},{4,20},{20... | collective-permute-start | bytes 147464 | tf_op jit(solution)/shard_map/ppermute | solution.py:341
  23.8 3.4 %shard_map.102 = (f32[64,1024]{1,0:T(8,128)S(1)}, bf16[4,16,640]{2,1,0:T(8,128)(2,1)S(1)}, bf16[2,16,4,1024]{3,2,1,0:T(4,128)(2,1)}) custom-call(s32[1]{0:T(128)} %bitcast.row_ref, s32[1]{0:T(128)} %bitcast.3.parity_ref, s32[2]{0:T(128)S(1)} %copy-done.1, s32[2,2,8]{2,1,0:T(2,128)S(1)} %bitcast.7, s32[2,8]{1,0:T(2,128)S(1)} %copy-done, ...), custom_call_target="tpu_custom_call" | custom-call | flops 402653184 | bytes 3461328 | tf_op jit(solution)/shard_map/pallas_call | solution.py:297
  27.2 0.0 collective-permute-done.4.got_ref
  27.2 2.4 %shard_map.103 = (bf16[4,8,2560]{2,1,0:T(8,128)(2,1)}, bf16[2,16,4,1024]{3,2,1,0:T(4,128)(2,1)}) custom-call(s32[1]{0:T(128)} %bitcast.row_ref, s32[2]{0:T(128)S(1)} %copy-done.1, s32[2,8]{1,0:T(2,128)S(1)} %copy-done, bf16[8,128,384]{2,1,0:T(8,128)(2,1)S(1)} %get-tuple-element.25.w0_ref.w_ref, ...), custom_call_target="tpu_custom_call", output_to_operand_aliasing={{1}: (8, {})} | custom-call | flops 201326592 | bytes 2752588 | tf_op jit(solution)/shard_map/pallas_call | solution.py:297
  (1 shorter events, 0.0 us)
Async XLA Ops:
  1.5 9.4 %collective-permute-start = (bf16[4,8,1024]{2,1,0:T(8,128)(2,1)S(1)}, bf16[4,8,1024]{2,1,0:T(8,128)(2,1)S(1)}, u32[]{:S(2)}, u32[]{:S(2)}) collective-permute-start(bf16[4,8,1024]{2,1,0:T(8,128)(2,1)S(1)} %get-tuple-element.31), channel_id=1, source_target_pairs={{0,1},{1,0},{2,3},{3,2},{4,5},{5,4},{6,7},{7,6},{8,9},{9,8},{10,11... | collective-permute-start | bytes 196616 | tf_op jit(solution)/shard_map/ppermute | solution.py:337
  2.1 8.9 %collective-permute-start.1 = (bf16[4,8,1024]{2,1,0:T(8,128)(2,1)S(1)}, bf16[4,8,1024]{2,1,0:T(8,128)(2,1)S(1)}, u32[]{:S(2)}, u32[]{:S(2)}) collective-permute-start(bf16[4,8,1024]{2,1,0:T(8,128)(2,1)S(1)} %get-tuple-element.32), channel_id=1, source_target_pairs={{0,15},{1,2},{2,1},{3,4},{4,3},{5,6},{6,5},{7,8},{8,7},{9,10},{10,... | collective-permute-start | bytes 196616 | tf_op jit(solution)/shard_map/ppermute | solution.py:337
  7.7 0.7 %copy-start.1 = (s32[2]{0:T(128)S(1)}, s32[2]{0:T(128)}, u32[]{:S(2)}) copy-start(s32[2]{0:T(128)} %band_ref.13) | copy-start | bytes 28
  8.4 4.2 %copy-start = (s32[2,8]{1,0:T(2,128)S(1)}, s32[2,8]{1,0:T(2,128)}, u32[]{:S(2)}) copy-start(s32[2,8]{1,0:T(2,128)} %iidx_ref.11) | copy-start | bytes 196
  8.4 4.2 %copy-start.2 = (s32[2,8,2]{1,2,0:T(2,128)S(1)}, s32[2,8,2]{1,2,0:T(2,128)}, u32[]{:S(2)}) copy-start(s32[2,8,2]{1,2,0:T(2,128)} %param.11) | copy-start | bytes 388
  11.0 4.2 %collective-permute-start.2 = (bf16[2,16,896]{2,1,0:T(8,128)(2,1)S(1)}, bf16[2,16,896]{2,1,0:T(8,128)(2,1)S(1)}, u32[]{:S(2)}, u32[]{:S(2)}) collective-permute-start(bf16[2,16,896]{2,1,0:T(8,128)(2,1)S(1)} %shard_map.98), channel_id=1, source_target_pairs={{0,16},{16,0},{1,17},{17,1},{2,18},{18,2},{3,19},{19,3},{4,20},{20... | collective-permute-start | bytes 172040 | tf_op jit(solution)/shard_map/ppermute | solution.py:341
  16.6 4.5 %collective-permute-start.3 = (bf16[2,16,768]{2,1,0:T(8,128)(2,1)S(1)}, bf16[2,16,768]{2,1,0:T(8,128)(2,1)S(1)}, u32[]{:S(2)}, u32[]{:S(2)}) collective-permute-start(bf16[2,16,768]{2,1,0:T(8,128)(2,1)S(1)} %get-tuple-element.39), channel_id=1, source_target_pairs={{0,16},{16,0},{1,17},{17,1},{2,18},{18,2},{3,19},{19,3},{4,20},{20... | collective-permute-start | bytes 147464 | tf_op jit(solution)/shard_map/ppermute | solution.py:341
  22.4 4.8 %collective-permute-start.4 = (bf16[2,16,768]{2,1,0:T(8,128)(2,1)S(1)}, bf16[2,16,768]{2,1,0:T(8,128)(2,1)S(1)}, u32[]{:S(2)}, u32[]{:S(2)}) collective-permute-start(bf16[2,16,768]{2,1,0:T(8,128)(2,1)S(1)} %get-tuple-element.45), channel_id=1, source_target_pairs={{0,16},{16,0},{1,17},{17,1},{2,18},{18,2},{3,19},{19,3},{4,20},{20... | collective-permute-start | bytes 147464 | tf_op jit(solution)/shard_map/ppermute | solution.py:341

commit v2 on v1

--- a/solution.py
+++ b/solution.py
@@ -52,7 +52,7 @@
             out[2 + d // 4, at : at + MEM, lane : lane + HALF] = rows[d]
 
 
-def setup_kernel(row_ref, band_ref, field_hbm, state_hbm, coup_hbm, inp_hbm, read_hbm, own_ref, s0_ref, s1_ref, w0_ref, w1_ref, read_ref, field_ref, state_ref, sems):
+def own_kernel(row_ref, field_hbm, state_hbm, coup_hbm, inp_hbm, own_ref, s0_ref, s1_ref, w_ref, field_ref, state_ref, sems):
     copies = []
 
     def start(src, dst):
@@ -61,12 +61,9 @@
 
     start(field_hbm, field_ref)
     start(state_hbm, state_ref)
-    for slot, w_ref in enumerate((w0_ref, w1_ref)):
-        band = band_ref[row_of(slot, row_ref)]
-        for k in range(2):
-            start(coup_hbm.at[band, :, k], w_ref.at[:, :, k * BLK : (k + 1) * BLK])
-        start(inp_hbm.at[band], w_ref.at[:, :, 2 * BLK :])
-    start(read_hbm.at[0], read_ref)
+    for k in range(2):
+        start(coup_hbm.at[:, :, k], w_ref.at[:, :, :, k * BLK : (k + 1) * BLK])
+    start(inp_hbm, w_ref.at[:, :, :, 2 * BLK :])
     chunks = field_ref.shape[2] // CHUNK
     copies[0].wait()
     tiles = []
@@ -146,10 +143,10 @@
     for k in range(2):
         pieces.append(s_ref[:, pl.ds(pl.multiple_of(cidx_ref[band, k, b] * BLK, BLK), BLK)])
     pieces.append(in_ref[:, pl.ds(pl.multiple_of(iidx_ref[band, b] * BLK, BLK), BLK)])
-    return lax.dot_general(jnp.concatenate(pieces, axis=1), w_ref[b], NT, preferred_element_type=F32)
-
-
-def shadow_kernel(first, last, slots, row_ref, parity_ref, band_ref, cidx_ref, iidx_ref, w0_ref, w1_ref, read_ref, *rest):
+    return lax.dot_general(jnp.concatenate(pieces, axis=1), w_ref[band, b], NT, preferred_element_type=F32)
+
+
+def shadow_kernel(first, last, slots, row_ref, parity_ref, band_ref, cidx_ref, iidx_ref, *rest):
     rest = list(rest)
 
     def take(n):
@@ -157,16 +154,28 @@
         del rest[:n]
         return got
 
+    w_ref = take(1)[0]
     if first:
-        own_ref, s0_ref, s1_ref, first_ref, second_ref = take(5)
+        read_hbm, own_ref, s0_ref, s1_ref, first_ref, second_ref = take(6)
     else:
+        read_ref = take(1)[0]
         edge_refs, s_refs = take(slots), take(slots)
         far_refs = take(2 * (2 - slots))
     pre_refs = take(slots)
     out_far = take(2 * (2 - slots))
-    xs_ref, in_ref, sc0_ref, sc1_ref, pre_ref = take(5)
+    if first:
+        read_ref = take(1)[0]
+    xs_ref, in_ref = take(2)
     rows_at = [row_of(0, row_ref), row_of(1, row_ref)]
-    w_refs = [w0_ref, w1_ref]
+    waits = {}
+    if first:
+        sc0_ref, sc1_ref, sem = take(3)
+        waits["read"] = pltpu.make_async_copy(read_hbm.at[0], read_ref, sem)
+        waits["read"].start()
+
+    def ready(name):
+        if name in waits:
+            waits.pop(name).wait()
 
     for k in range(2):
         xs_ref[k] = jnp.zeros(xs_ref.shape[1:], F32)
@@ -204,46 +213,49 @@
                 xs_ref[2 + 4 * rows_at[1] + d] = far_refs[0][d].astype(F32)
             s_refs = [s_refs[0], far_refs[1]]
 
+    far = []
     for slot in (1, 0):
         r = rows_at[slot]
         band = band_ref[r]
         in_ref[...] = windows([xs_ref[4 * r + d] for d in range(8)], False)
         blocks = iidx_ref.shape[1]
-        pres = [block_pre(b, band, s_refs[slot], in_ref, cidx_ref, iidx_ref, w_refs[slot]) for b in range(blocks)]
-        if slot < slots:
-            if not last:
-                for b in range(blocks):
-                    pre_refs[slot][:, b * BLK : (b + 1) * BLK] = pres[b]
-            else:
-                for b in range(blocks):
-                    pre_ref[:, b * BLK : (b + 1) * BLK] = pres[b]
-                per = pre_ref.shape[0] // 4
-                short = per - 2 * MEM
-                for res in range(4):
-                    pre_refs[slot][res * short : (res + 1) * short] = pre_ref[res * per + MEM : (res + 1) * per - MEM]
-            continue
-        state = jnp.concatenate([jnp.tanh(p).astype(BF) for p in pres], axis=1)
+        pres = [block_pre(b, band, s_refs[slot], in_ref, cidx_ref, iidx_ref, w_ref) for b in range(blocks)]
+        if slot >= slots:
+            far = [jnp.concatenate([jnp.tanh(p).astype(BF) for p in pres], axis=1)]
+            if last:
+                stage_ref, sem = take(2)
+                waits["out"] = put_states(r, far[0], MEM, stage_ref, out_far[1], sem)
+        elif not last:
+            for b in range(blocks):
+                pre_refs[slot][:, b * BLK : (b + 1) * BLK] = pres[b]
+        else:
+            pre_ref = take(1)[0]
+            for b in range(blocks):
+                pre_ref[:, b * BLK : (b + 1) * BLK] = pres[b]
+            per = pre_ref.shape[0] // 4
+            short = per - 2 * MEM
+            for res in range(4):
+                pre_refs[slot][res * short : (res + 1) * short] = pre_ref[res * per + MEM : (res + 1) * per - MEM]
+    ready("read")
+    for state in far:
         pred = lax.dot_general(state, read_ref[...], NT, preferred_element_type=F32)
+        for d in range(4):
+            lat = latitude(pred, d).astype(BF)
+            out_far[0][d] = lat[MEM:-MEM] if last else lat
         if not last:
-            for d in range(4):
-                out_far[0][d] = latitude(pred, d).astype(BF)
             out_far[1][...] = state
-            continue
-        for d in range(4):
-            out_far[0][d] = latitude(pred, d)[MEM:-MEM].astype(BF)
-        stage_ref, sem = take(2)
-        per = state.shape[0] // 4
-        put_states(r, state, per, MEM, stage_ref, out_far[1], sem)
-
-
-def put_states(r, state, per, skip, stage_ref, states_hbm, sem):
+    ready("out")
+
+
+def put_states(r, state, skip, stage_ref, states_hbm, sem):
+    per = state.shape[0] // 4
     for res in range(4):
         for q in range((per - 2 * skip) // MEM):
             at = res * per + skip + q * MEM
             stage_ref[4 * q + res] = state[at : at + MEM]
     copy = pltpu.make_async_copy(stage_ref, states_hbm.at[r], sem)
     copy.start()
-    copy.wait()
+    return copy
 
 
 def late_kernel(slot, last, final, row_ref, band_ref, iidx_ref, w_ref, read_ref, pre_ref, got_ref, *rest):
@@ -256,7 +268,7 @@
         k = iidx_ref[band, b] - 15 * r
         used = jnp.logical_and(k >= 0, k < 5)
         at = pl.multiple_of(jnp.where(used, k, 0) * BLK, BLK)
-        term = lax.dot_general(in_ref[:, pl.ds(at, BLK)], w_ref[b, :, 2 * BLK :], NT, preferred_element_type=F32)
+        term = lax.dot_general(in_ref[:, pl.ds(at, BLK)], w_ref[band, b, :, 2 * BLK :], NT, preferred_element_type=F32)
         pre = pre_ref[:, b * BLK : (b + 1) * BLK] + jnp.where(used, term, 0.0)
         parts.append(jnp.tanh(pre).astype(BF))
     state = jnp.concatenate(parts, axis=1)
@@ -270,16 +282,18 @@
             pack(row, msg_ref, d)
             edge_ref[d] = row.astype(BF)
         return
+    if not final:
+        lats_ref, states_hbm, stage_ref, sem = rest[:4]
+    else:
+        other_ref, _, field_hbm, states_hbm, stage_ref, sem, field_ref, field_sem = rest[:8]
+    copy = put_states(r, state, 0, stage_ref, states_hbm, sem)
     pred = lax.dot_general(state, read_ref[...], NT, preferred_element_type=F32)
     mine = [latitude(pred, d) for d in range(4)]
-    per = state.shape[0] // 4
     if not final:
-        lats_ref, states_hbm, stage_ref, sem = rest[:4]
         for d in range(4):
             lats_ref[d] = mine[d].astype(BF)
-        put_states(r, state, per, 0, stage_ref, states_hbm, sem)
+        copy.wait()
         return
-    other_ref, _, field_ref, states_hbm, stage_ref, sem = rest[:6]
     other = [other_ref[d].astype(F32) for d in range(4)]
     low = r == 0
     rows = [jnp.where(low, mine[d], other[d])[None] for d in range(4)]
@@ -288,7 +302,10 @@
     for q in range(field_ref.shape[2] // CHUNK):
         for m in range(MEM):
             field_ref[m, :, q * CHUNK : (q + 1) * CHUNK] = tiles[q * MEM + m]
-    put_states(r, state, per, 0, stage_ref, states_hbm, sem)
+    out = pltpu.make_async_copy(field_ref, field_hbm, field_sem)
+    out.start()
+    copy.wait()
+    out.wait()
 
 
 def call(kernel, out_shape, out_specs, scratch, operands, flops=0, aliases=None):
@@ -344,7 +361,7 @@
         return [down, up]
 
     row = ((1 - lat_at if swap else lat_at * 0).reshape(1), SM)
-    parity = ((lon_at % 2).reshape(1), SM)
+    parity = (((lon_at + 1) % 2).reshape(1), SM)
     band, cidx, iidx = (region_band, SM), (coupling_index.transpose(0, 2, 1), SM), (input_index, SM)
     flops = 2 * rows * units * (3 * BLK + outs)
 
@@ -355,25 +372,22 @@
         [vm((2, MEM, 8, HALF)), vm((2, region_rows, 2, MEM, units)), pltpu.SemaphoreType.DMA((4,))],
         [parity, (field_state, HB), (reservoir_state, HB)],
     )
-    second = trade(mail[1], 1)
-    first = trade(mail[0], 0)
-    own, s0, s1, w0, w1, read = call(
-        setup_kernel,
-        [bf(8, own_rows, CHUNK), bf(short, units), bf(short, units), bf(blocks, BLK, 3 * BLK), bf(blocks, BLK, 3 * BLK), bf(outs, units)],
-        [VM] * 6,
-        [vm(field_state.shape), vm(reservoir_state.shape), pltpu.SemaphoreType.DMA((9,))],
+    first = trade(mail[0], 1)
+    second = trade(mail[1], 0)
+    own, s0, s1, w = call(
+        own_kernel,
+        [bf(8, own_rows, CHUNK), bf(short, units), bf(short, units), bf(bands, blocks, BLK, 3 * BLK)],
+        [VM] * 4,
+        [vm(field_state.shape), vm(reservoir_state.shape), pltpu.SemaphoreType.DMA((5,))],
         [
             row,
-            band,
             (field_state, HB),
             (reservoir_state, HB),
             (coupling_blocks.reshape(bands, blocks, 2, BLK, BLK), HB),
             (input_blocks.reshape(bands, blocks, BLK, BLK), HB),
-            (readout, HB),
         ],
         flops,
     )
-    weights = [(w0, VM), (w1, VM), (read, VM)]
     sent = call(
         functools.partial(first_edge_kernel, slots),
         [bf(2, own_rows, CHUNK + HALF // 2)] * slots,
@@ -381,7 +395,8 @@
         [],
         [parity, row, (own, VM), (first, VM), (second, VM)],
     )
-    source = [(x, VM) for x in (own, s0, s1, first, second)]
+    weights = [(w, VM)]
+    source = weights + [(readout, HB)] + [(x, VM) for x in (own, s0, s1, first, second)]
     states_shape = bf(region_rows, regions, MEM, units)
     stage = [vm((regions, MEM, units)), pltpu.SemaphoreType.DMA]
 
@@ -391,23 +406,31 @@
         pre_rows = short if last else rows
         out = [jax.ShapeDtypeStruct((pre_rows, units), F32)] * slots
         specs = [VM] * slots
-        scratch = [vm((12, wide, CHUNK), F32), vm((rows, 16 * CELL)), vm((rows, units)), vm((rows, units)), vm((rows, units), F32)]
+        scratch = [vm((12, wide, CHUNK), F32), vm((rows, 16 * CELL))]
         if swap:
             out += [bf(4, own_rows if last else wide, CHUNK), states_shape if last else bf(rows, units)]
             specs += [VM, HB if last else VM]
             scratch += stage if last else []
+        if last:
+            scratch += [vm((rows, units), F32)] * slots
+        if step == 0:
+            out += [bf(outs, units)]
+            specs += [VM]
+            scratch += [vm((rows, units))] * 2 + [pltpu.SemaphoreType.DMA]
         shadow = call(
             functools.partial(shadow_kernel, step == 0, last, slots),
             out,
             specs,
             scratch,
-            [row, parity, band, cidx, iidx] + weights + source,
+            [row, parity, band, cidx, iidx] + source,
             2 * flops,
         )
-        far = shadow[slots:]
+        far = shadow[slots : slots + 2 * (2 - slots)]
+        if step == 0:
+            weights.append((shadow[-1], VM))
         sent, edges, states = [None] * slots, [None] * slots, [None] * slots
         for slot in reversed(range(slots)):
-            operands = [row, band, iidx, weights[slot], weights[2], (shadow[slot], VM), (got[slot], VM)]
+            operands = [row, band, iidx] + weights + [ (shadow[slot], VM), (got[slot], VM)]
             inputs = [vm((pre_rows, 4 * CELL))]
             if not last:
                 sent[slot], edges[slot], states[slot] = call(
@@ -431,13 +454,13 @@
                 return call(
                     functools.partial(late_kernel, slot, True, True),
                     [bf(MEM, 8, regions * CELL), states_shape],
-                    [VM, HB],
-                    stage + inputs,
+                    [HB, HB],
+                    stage + [vm((MEM, 8, regions * CELL)), pltpu.SemaphoreType.DMA] + inputs,
                     operands + [(far[0], VM), (far[1], HB)],
                     flops,
                     {len(operands) + 1: 1},
                 )
-        source = [(x, VM) for x in edges + states + list(far)]
+        source = weights + [(x, VM) for x in edges + states + list(far)]
 
 
 def solution(mesh):

time: 29.8 us -> 28.1 us (0.943)
  starting transfers between devices: 10.9 us -> 8.94 us
  local copies, waits for them, and re-layouts: 0.66 us -> 0.01 us
  waiting for transfers between devices: 0.64 us -> 1.17 us
  Pallas kernels: 16.7 us -> 17 us
    ppermute x3, starting transfers between devices: 4.69 us -> 3.43 us  [across(): return [lax.ppermute(xs[0], 'lat', [(0, 1), (1, 0)])]]
    ppermute x2, starting transfers between devices: 6.18 us -> 5.51 us  [trade(): return lax.ppermute(x, 'lon', pairs)]
    unnamed x6, local copies, waits for them, and re-layouts: 0.66 us -> 0.01 us
    ppermute x2, waiting for transfers between devices: 0.01 us -> 0.37 us  [trade(): return lax.ppermute(x, 'lon', pairs)]
  transfers between devices with their start and end apart: 5 -> 5, of which waited for: 2 -> 3; matrix products, arithmetic and copies ran while one was open for 0% -> 0% of each run, Pallas kernels for 36% -> 40%
where the time goes in v2:
time: 28.1 us; the launch traced here: 27.8 us
  Pallas kernels  17 us (60%)
  starting transfers between devices  8.94 us (32%)
  waiting for transfers between devices  1.17 us (4%)
  between operations  0.74 us (3%)
    pallas_call x9, Pallas kernels, call(): pl.pallas_call(kernel, out_shape=out_shape, in_specs=[s for _, s in opera...  17 us
    ppermute x2, starting transfers between devices, trade(): return lax.ppermute(x, 'lon', pairs)  5.51 us
    ppermute x3, starting transfers between devices, across(): return [lax.ppermute(xs[0], 'lat', [(0, 1), (1, 0)])]  3.43 us
    ppermute x3, waiting for transfers between devices, across(): return [lax.ppermute(xs[0], 'lat', [(0, 1), (1, 0)])]  0.8 us
  transfers between devices with their start and end apart: 5, of which 3 were waited for; matrix products, arithmetic and copies ran while one was open for 0% of the time, Pallas kernels for 40%

profile of v2, /device:TPU:0, one launch (start us, length us, event | category | flops | bytes accessed | tf_op | source)
XLA Modules:
  0.0 27.8 jit_solution(3751488343157702447)
XLA Ops:
  0.6 0.0 copy-start
  0.7 0.0 copy-start.1
  0.7 0.0 copy-start.2
  0.7 0.9 %shard_map.96 = (bf16[4,8,1024]{2,1,0:T(8,128)(2,1)S(1)}, bf16[4,8,1024]{2,1,0:T(8,128)(2,1)S(1)}) custom-call(s32[1]{0:T(128)} %bitcast.3.parity_ref, bf16[4,8,2560]{2,1,0:T(8,128)(2,1)} %field_hbm.3, bf16[2,16,4,1024]{3,2,1,0:T(4,128)(2,1)} %state_hbm.3), custom_call_target="tpu_custom_call" | custom-call | bytes 425988 | tf_op jit(solution)/shard_map/pallas_call | solution.py:314
  1.6 5.5 %collective-permute-start = (bf16[4,8,1024]{2,1,0:T(8,128)(2,1)S(1)}, bf16[4,8,1024]{2,1,0:T(8,128)(2,1)S(1)}, u32[]{:S(2)}, u32[]{:S(2)}) collective-permute-start(bf16[4,8,1024]{2,1,0:T(8,128)(2,1)S(1)} %get-tuple-element.28), channel_id=1, source_target_pairs={{0,15},{1,2},{2,1},{3,4},{4,3},{5,6},{6,5},{7,8},{8,7},{9,10},{10,... | collective-permute-start | bytes 196616 | tf_op jit(solution)/shard_map/ppermute | solution.py:354
  7.1 0.0 collective-permute-start.1
  7.1 1.6 %shard_map.95 = (bf16[8,16,640]{2,1,0:T(8,128)(2,1)S(1)}, bf16[64,1024]{1,0:T(8,128)(2,1)S(1)}, bf16[64,1024]{1,0:T(8,128)(2,1)S(1)}, bf16[2,8,128,384]{3,2,1,0:T(8,128)(2,1)S(1)}) custom-call(s32[1]{0:T(128)} %bitcast.row_ref, bf16[4,8,2560]{2,1,0:T(8,128)(2,1)} %field_hbm.3, bf16[2,16,4,1024]{3,2,1,0:T(4,128)(2,1)} %state_hbm.3, ...), custom_call_target="tpu_custom_call" | custom-call | flops 201326592 | bytes 1998852 | tf_op jit(solution)/shard_map/pallas_call | solution.py:314
  8.7 0.4 %collective-permute-done.rest_5_.first_ref = bf16[4,8,1024]{2,1,0:T(8,128)(2,1)S(1)} collective-permute-done((bf16[4,8,1024]{2,1,0:T(8,128)(2,1)S(1)}, bf16[4,8,1024]{2,1,0:T(8,128)(2,1)S(1)}, u32[]{:S(2)}, u32[]{:S(2)}) %collective-permute-start) | collective-permute-done | bytes 65568 | tf_op jit(solution)/shard_map/ppermute | solution.py:354
  9.0 0.0 collective-permute-done.1.rest_6_.second_ref
  9.1 2.0 %collective-permute-start.2 = (bf16[2,16,896]{2,1,0:T(8,128)(2,1)S(1)}, bf16[2,16,896]{2,1,0:T(8,128)(2,1)S(1)}, u32[]{:S(2)}, u32[]{:S(2)}) collective-permute-start(bf16[2,16,896]{2,1,0:T(8,128)(2,1)S(1)} %shard_map.98), channel_id=1, source_target_pairs={{0,16},{16,0},{1,17},{17,1},{2,18},{18,2},{3,19},{19,3},{4,20},{20... | collective-permute-start | bytes 172040 | tf_op jit(solution)/shard_map/ppermute | solution.py:358
  11.1 0.0 copy-done
  11.1 0.0 copy-done.1
  11.1 0.0 copy-done.2
  11.1 3.5 %shard_map.97 = (f32[96,1024]{1,0:T(8,128)S(1)}, bf16[4,24,640]{2,1,0:T(8,128)(2,1)S(1)}, bf16[96,1024]{1,0:T(8,128)(2,1)S(1)}, bf16[640,1024]{1,0:T(8,128)(2,1)S(1)}) custom-call(s32[1]{0:T(128)} %bitcast.row_ref, s32[1]{0:T(128)} %bitcast.3.parity_ref, s32[2]{0:T(128)S(1)} %copy-done.1, s32[2,2,8]{2,1,0:T(2,128)S(1)} %bitcast.5, s32[2,8]{1,0:T(2,128)S(1)} %copy-done, ...), custom_call_target="tpu_custom_call" | custom-call | flops 402653184 | bytes 3440848 | tf_op jit(solution)/shard_map/pallas_call | solution.py:314
  14.6 0.0 collective-permute-done.2.got_ref
  14.6 1.3 %shard_map.99 = (bf16[2,16,768]{2,1,0:T(8,128)(2,1)S(1)}, bf16[2,24,640]{2,1,0:T(8,128)(2,1)S(1)}, bf16[96,1024]{1,0:T(8,128)(2,1)S(1)}) custom-call(s32[1]{0:T(128)} %bitcast.row_ref, s32[2]{0:T(128)S(1)} %copy-done.1, s32[2,8]{1,0:T(2,128)S(1)} %copy-done, bf16[2,8,128,384]{3,2,1,0:T(8,128)(2,1)S(1)} %get-tuple-element.24.rest_0_.w_ref, ...), custom_call_target="tpu_custom_call" | custom-call | flops 201326592 | bytes 3334220 | tf_op jit(solution)/shard_map/pallas_call | solution.py:314
  16.0 0.7 %collective-permute-start.3 = (bf16[2,16,768]{2,1,0:T(8,128)(2,1)S(1)}, bf16[2,16,768]{2,1,0:T(8,128)(2,1)S(1)}, u32[]{:S(2)}, u32[]{:S(2)}) collective-permute-start(bf16[2,16,768]{2,1,0:T(8,128)(2,1)S(1)} %get-tuple-element.37), channel_id=1, source_target_pairs={{0,16},{16,0},{1,17},{17,1},{2,18},{18,2},{3,19},{19,3},{4,20},{20... | collective-permute-start | bytes 147464 | tf_op jit(solution)/shard_map/ppermute | solution.py:358
  16.6 2.7 %shard_map.100 = (f32[96,1024]{1,0:T(8,128)S(1)}, bf16[4,24,640]{2,1,0:T(8,128)(2,1)S(1)}, bf16[96,1024]{1,0:T(8,128)(2,1)S(1)}) custom-call(s32[1]{0:T(128)} %bitcast.row_ref, s32[1]{0:T(128)} %bitcast.3.parity_ref, s32[2]{0:T(128)S(1)} %copy-done.1, s32[2,2,8]{2,1,0:T(2,128)S(1)} %bitcast.6, s32[2,8]{1,0:T(2,128)S(1)} %copy-done, ...), custom_call_target="tpu_custom_call" | custom-call | flops 402653184 | bytes 3461328 | tf_op jit(solution)/shard_map/pallas_call | solution.py:314
  19.4 0.7 %collective-permute-done.3.got_ref = bf16[2,16,768]{2,1,0:T(8,128)(2,1)S(1)} collective-permute-done((bf16[2,16,768]{2,1,0:T(8,128)(2,1)S(1)}, bf16[2,16,768]{2,1,0:T(8,128)(2,1)S(1)}, u32[]{:S(2)}, u32[]{:S(2)}) %collective-permute-start.3) | collective-permute-done | bytes 49184 | tf_op jit(solution)/shard_map/ppermute | solution.py:358
  20.1 1.3 %shard_map.101 = (bf16[2,16,768]{2,1,0:T(8,128)(2,1)S(1)}, bf16[2,24,640]{2,1,0:T(8,128)(2,1)S(1)}, bf16[96,1024]{1,0:T(8,128)(2,1)S(1)}) custom-call(s32[1]{0:T(128)} %bitcast.row_ref, s32[2]{0:T(128)S(1)} %copy-done.1, s32[2,8]{1,0:T(2,128)S(1)} %copy-done, bf16[2,8,128,384]{3,2,1,0:T(8,128)(2,1)S(1)} %get-tuple-element.24.rest_0_.w_ref, ...), custom_call_target="tpu_custom_call" | custom-call | flops 201326592 | bytes 3326028 | tf_op jit(solution)/shard_map/pallas_call | solution.py:314
  21.4 0.7 %collective-permute-start.4 = (bf16[2,16,768]{2,1,0:T(8,128)(2,1)S(1)}, bf16[2,16,768]{2,1,0:T(8,128)(2,1)S(1)}, u32[]{:S(2)}, u32[]{:S(2)}) collective-permute-start(bf16[2,16,768]{2,1,0:T(8,128)(2,1)S(1)} %get-tuple-element.43), channel_id=1, source_target_pairs={{0,16},{16,0},{1,17},{17,1},{2,18},{18,2},{3,19},{19,3},{4,20},{20... | collective-permute-start | bytes 147464 | tf_op jit(solution)/shard_map/ppermute | solution.py:358
  22.2 3.3 %shard_map.102 = (f32[64,1024]{1,0:T(8,128)S(1)}, bf16[4,16,640]{2,1,0:T(8,128)(2,1)S(1)}, bf16[2,16,4,1024]{3,2,1,0:T(4,128)(2,1)}) custom-call(s32[1]{0:T(128)} %bitcast.row_ref, s32[1]{0:T(128)} %bitcast.3.parity_ref, s32[2]{0:T(128)S(1)} %copy-done.1, s32[2,2,8]{2,1,0:T(2,128)S(1)} %bitcast.7, s32[2,8]{1,0:T(2,128)S(1)} %copy-done, ...), custom_call_target="tpu_custom_call" | custom-call | flops 402653184 | bytes 3461328 | tf_op jit(solution)/shard_map/pallas_call | solution.py:314
  25.6 0.1 collective-permute-done.4.got_ref
  25.6 2.2 %shard_map.103 = (bf16[4,8,2560]{2,1,0:T(8,128)(2,1)}, bf16[2,16,4,1024]{3,2,1,0:T(4,128)(2,1)}) custom-call(s32[1]{0:T(128)} %bitcast.row_ref, s32[2]{0:T(128)S(1)} %copy-done.1, s32[2,8]{1,0:T(2,128)S(1)} %copy-done, bf16[2,8,128,384]{3,2,1,0:T(8,128)(2,1)S(1)} %get-tuple-element.24.rest_0_.w_ref, ...), custom_call_target="tpu_custom_call", output_to_operand_aliasing={{1}: (8, {})} | custom-call | flops 201326592 | bytes 3539020 | tf_op jit(solution)/shard_map/pallas_call | solution.py:314
  (1 shorter events, 0.0 us)
Async XLA Ops:
  0.6 10.4 %copy-start = (s32[2,8]{1,0:T(2,128)S(1)}, s32[2,8]{1,0:T(2,128)}, u32[]{:S(2)}) copy-start(s32[2,8]{1,0:T(2,128)} %iidx_ref.11) | copy-start | bytes 196
  0.7 10.4 %copy-start.1 = (s32[2]{0:T(128)S(1)}, s32[2]{0:T(128)}, u32[]{:S(2)}) copy-start(s32[2]{0:T(128)} %band_ref.11) | copy-start | bytes 28
  0.7 10.4 %copy-start.2 = (s32[2,8,2]{1,2,0:T(2,128)S(1)}, s32[2,8,2]{1,2,0:T(2,128)}, u32[]{:S(2)}) copy-start(s32[2,8,2]{1,2,0:T(2,128)} %param.11) | copy-start | bytes 388
  1.6 7.5 %collective-permute-start = (bf16[4,8,1024]{2,1,0:T(8,128)(2,1)S(1)}, bf16[4,8,1024]{2,1,0:T(8,128)(2,1)S(1)}, u32[]{:S(2)}, u32[]{:S(2)}) collective-permute-start(bf16[4,8,1024]{2,1,0:T(8,128)(2,1)S(1)} %get-tuple-element.28), channel_id=1, source_target_pairs={{0,15},{1,2},{2,1},{3,4},{4,3},{5,6},{6,5},{7,8},{8,7},{9,10},{10,... | collective-permute-start | bytes 196616 | tf_op jit(solution)/shard_map/ppermute | solution.py:354
  7.1 2.0 %collective-permute-start.1 = (bf16[4,8,1024]{2,1,0:T(8,128)(2,1)S(1)}, bf16[4,8,1024]{2,1,0:T(8,128)(2,1)S(1)}, u32[]{:S(2)}, u32[]{:S(2)}) collective-permute-start(bf16[4,8,1024]{2,1,0:T(8,128)(2,1)S(1)} %get-tuple-element.29), channel_id=1, source_target_pairs={{0,1},{1,0},{2,3},{3,2},{4,5},{5,4},{6,7},{7,6},{8,9},{9,8},{10,11... | collective-permute-start | bytes 196616 | tf_op jit(solution)/shard_map/ppermute | solution.py:354
  9.1 5.6 %collective-permute-start.2 = (bf16[2,16,896]{2,1,0:T(8,128)(2,1)S(1)}, bf16[2,16,896]{2,1,0:T(8,128)(2,1)S(1)}, u32[]{:S(2)}, u32[]{:S(2)}) collective-permute-start(bf16[2,16,896]{2,1,0:T(8,128)(2,1)S(1)} %shard_map.98), channel_id=1, source_target_pairs={{0,16},{16,0},{1,17},{17,1},{2,18},{18,2},{3,19},{19,3},{4,20},{20... | collective-permute-start | bytes 172040 | tf_op jit(solution)/shard_map/ppermute | solution.py:358
  16.0 4.2 %collective-permute-start.3 = (bf16[2,16,768]{2,1,0:T(8,128)(2,1)S(1)}, bf16[2,16,768]{2,1,0:T(8,128)(2,1)S(1)}, u32[]{:S(2)}, u32[]{:S(2)}) collective-permute-start(bf16[2,16,768]{2,1,0:T(8,128)(2,1)S(1)} %get-tuple-element.37), channel_id=1, source_target_pairs={{0,16},{16,0},{1,17},{17,1},{2,18},{18,2},{3,19},{19,3},{4,20},{20... | collective-permute-start | bytes 147464 | tf_op jit(solution)/shard_map/ppermute | solution.py:358
  21.4 4.2 %collective-permute-start.4 = (bf16[2,16,768]{2,1,0:T(8,128)(2,1)S(1)}, bf16[2,16,768]{2,1,0:T(8,128)(2,1)S(1)}, u32[]{:S(2)}, u32[]{:S(2)}) collective-permute-start(bf16[2,16,768]{2,1,0:T(8,128)(2,1)S(1)} %get-tuple-element.43), channel_id=1, source_target_pairs={{0,16},{16,0},{1,17},{17,1},{2,18},{18,2},{3,19},{19,3},{4,20},{20... | collective-permute-start | bytes 147464 | tf_op jit(solution)/shard_map/ppermute | solution.py:358

commit v3 on v2

--- a/solution.py
+++ b/solution.py
@@ -138,11 +138,22 @@
     return jnp.concatenate([pred[res * per : (res + 1) * per, d * CELL : (d + 1) * CELL] for res in range(4)], axis=1)
 
 
-def block_pre(b, band, s_ref, in_ref, cidx_ref, iidx_ref, w_ref):
+def of_band(band, values, *at):
+    got = values[(0, *at)]
+    for g in range(1, values.shape[0]):
+        got = jnp.where(band == g, values[(g, *at)], got)
+    return got
+
+
+def block_at(index, ref):
+    return pl.multiple_of(jnp.clip(index, 0, ref.shape[1] // BLK - 1) * BLK, BLK)
+
+
+def block_pre(b, band, s_ref, in_ref, cidx, iidx, w_ref):
     pieces = []
     for k in range(2):
-        pieces.append(s_ref[:, pl.ds(pl.multiple_of(cidx_ref[band, k, b] * BLK, BLK), BLK)])
-    pieces.append(in_ref[:, pl.ds(pl.multiple_of(iidx_ref[band, b] * BLK, BLK), BLK)])
+        pieces.append(s_ref[:, pl.ds(block_at(of_band(band, cidx, k, b), s_ref), BLK)])
+    pieces.append(in_ref[:, pl.ds(block_at(of_band(band, iidx, b), in_ref), BLK)])
     return lax.dot_general(jnp.concatenate(pieces, axis=1), w_ref[band, b], NT, preferred_element_type=F32)
 
 
@@ -214,12 +225,13 @@
             s_refs = [s_refs[0], far_refs[1]]
 
     far = []
+    bands, cidx, iidx = band_ref[...], cidx_ref[...], iidx_ref[...]
     for slot in (1, 0):
         r = rows_at[slot]
-        band = band_ref[r]
+        band = jnp.where(r == 0, bands[0], bands[1])
         in_ref[...] = windows([xs_ref[4 * r + d] for d in range(8)], False)
         blocks = iidx_ref.shape[1]
-        pres = [block_pre(b, band, s_refs[slot], in_ref, cidx_ref, iidx_ref, w_ref) for b in range(blocks)]
+        pres = [block_pre(b, band, s_refs[slot], in_ref, cidx, iidx, w_ref) for b in range(blocks)]
         if slot >= slots:
             far = [jnp.concatenate([jnp.tanh(p).astype(BF) for p in pres], axis=1)]
             if last:
@@ -260,12 +272,13 @@
 
 def late_kernel(slot, last, final, row_ref, band_ref, iidx_ref, w_ref, read_ref, pre_ref, got_ref, *rest):
     r = row_of(slot, row_ref)
-    band = band_ref[r]
+    bands, iidx = band_ref[...], iidx_ref[...]
+    band = jnp.where(r == 0, bands[0], bands[1])
     in_ref = rest[-1]
     in_ref[...] = windows([unpack(got_ref[k]) for k in range(2)], last)
     parts = []
     for b in range(iidx_ref.shape[1]):
-        k = iidx_ref[band, b] - 15 * r
+        k = of_band(band, iidx, b) - 15 * r
         used = jnp.logical_and(k >= 0, k < 5)
         at = pl.multiple_of(jnp.where(used, k, 0) * BLK, BLK)
         term = lax.dot_general(in_ref[:, pl.ds(at, BLK)], w_ref[band, b, :, 2 * BLK :], NT, preferred_element_type=F32)
@@ -362,7 +375,7 @@
 
     row = ((1 - lat_at if swap else lat_at * 0).reshape(1), SM)
     parity = (((lon_at + 1) % 2).reshape(1), SM)
-    band, cidx, iidx = (region_band, SM), (coupling_index.transpose(0, 2, 1), SM), (input_index, SM)
+    band, cidx, iidx = (region_band, VM), (coupling_index.transpose(0, 2, 1), VM), (input_index, VM)
     flops = 2 * rows * units * (3 * BLK + outs)
 
     mail = call(

time: 28.1 us -> 26 us (0.925)
  Pallas kernels: 17 us -> 13.7 us
  starting transfers between devices: 8.94 us -> 9.89 us
    pallas_call x9, Pallas kernels: 17 us -> 13.7 us  [call(): pl.pallas_call(kernel, out_shape=out_shape, in_specs=[s for _, s in opera...]
    ppermute x3, starting transfers between devices: 3.43 us -> 4.37 us  [across(): return [lax.ppermute(xs[0], 'lat', [(0, 1), (1, 0)])]]
  transfers between devices with their start and end apart: 5 -> 5, of which waited for: 3 -> 3; matrix products, arithmetic and copies ran while one was open for 0% -> 0% of each run, Pallas kernels for 40% -> 37%
where the time goes in v3:
time: 26 us; the launch traced here: 25.7 us
  Pallas kernels  13.7 us (53%)
  starting transfers between devices  9.89 us (38%)
  waiting for transfers between devices  1.4 us (5%)
  between operations  0.74 us (3%)
    pallas_call x9, Pallas kernels, call(): pl.pallas_call(kernel, out_shape=out_shape, in_specs=[s for _, s in opera...  13.7 us
    ppermute x2, starting transfers between devices, trade(): return lax.ppermute(x, 'lon', pairs)  5.51 us
    ppermute x3, starting transfers between devices, across(): return [lax.ppermute(xs[0], 'lat', [(0, 1), (1, 0)])]  4.37 us
    ppermute x3, waiting for transfers between devices, across(): return [lax.ppermute(xs[0], 'lat', [(0, 1), (1, 0)])]  1.03 us
  transfers between devices with their start and end apart: 5, of which 3 were waited for; matrix products, arithmetic and copies ran while one was open for 0% of the time, Pallas kernels for 37%

profile of v3, /device:TPU:0, one launch (start us, length us, event | category | flops | bytes accessed | tf_op | source)
XLA Modules:
  0.0 25.7 jit_solution(15725452742992653203)
XLA Ops:
  0.6 0.0 copy-start
  0.7 0.0 copy-start.1
  0.7 0.0 copy-start.2
  0.7 0.9 %shard_map.96 = (bf16[4,8,1024]{2,1,0:T(8,128)(2,1)S(1)}, bf16[4,8,1024]{2,1,0:T(8,128)(2,1)S(1)}) custom-call(s32[1]{0:T(128)} %bitcast.3.parity_ref, bf16[4,8,2560]{2,1,0:T(8,128)(2,1)} %field_hbm.3, bf16[2,16,4,1024]{3,2,1,0:T(4,128)(2,1)} %state_hbm.3), custom_call_target="tpu_custom_call" | custom-call | bytes 425988 | tf_op jit(solution)/shard_map/pallas_call | solution.py:327
  1.6 5.5 %collective-permute-start = (bf16[4,8,1024]{2,1,0:T(8,128)(2,1)S(1)}, bf16[4,8,1024]{2,1,0:T(8,128)(2,1)S(1)}, u32[]{:S(2)}, u32[]{:S(2)}) collective-permute-start(bf16[4,8,1024]{2,1,0:T(8,128)(2,1)S(1)} %get-tuple-element.28), channel_id=1, source_target_pairs={{0,15},{1,2},{2,1},{3,4},{4,3},{5,6},{6,5},{7,8},{8,7},{9,10},{10,... | collective-permute-start | bytes 196616 | tf_op jit(solution)/shard_map/ppermute | solution.py:367
  7.1 0.0 collective-permute-start.1
  7.1 1.6 %shard_map.95 = (bf16[8,16,640]{2,1,0:T(8,128)(2,1)S(1)}, bf16[64,1024]{1,0:T(8,128)(2,1)S(1)}, bf16[64,1024]{1,0:T(8,128)(2,1)S(1)}, bf16[2,8,128,384]{3,2,1,0:T(8,128)(2,1)S(1)}) custom-call(s32[1]{0:T(128)} %bitcast.row_ref, bf16[4,8,2560]{2,1,0:T(8,128)(2,1)} %field_hbm.3, bf16[2,16,4,1024]{3,2,1,0:T(4,128)(2,1)} %state_hbm.3, ...), custom_call_target="tpu_custom_call" | custom-call | flops 201326592 | bytes 1998852 | tf_op jit(solution)/shard_map/pallas_call | solution.py:327
  8.7 0.4 %collective-permute-done.rest_5_.first_ref = bf16[4,8,1024]{2,1,0:T(8,128)(2,1)S(1)} collective-permute-done((bf16[4,8,1024]{2,1,0:T(8,128)(2,1)S(1)}, bf16[4,8,1024]{2,1,0:T(8,128)(2,1)S(1)}, u32[]{:S(2)}, u32[]{:S(2)}) %collective-permute-start) | collective-permute-done | bytes 65568 | tf_op jit(solution)/shard_map/ppermute | solution.py:367
  9.0 0.0 collective-permute-done.1.rest_6_.second_ref
  9.1 2.0 %collective-permute-start.2 = (bf16[2,16,896]{2,1,0:T(8,128)(2,1)S(1)}, bf16[2,16,896]{2,1,0:T(8,128)(2,1)S(1)}, u32[]{:S(2)}, u32[]{:S(2)}) collective-permute-start(bf16[2,16,896]{2,1,0:T(8,128)(2,1)S(1)} %shard_map.98), channel_id=1, source_target_pairs={{0,16},{16,0},{1,17},{17,1},{2,18},{18,2},{3,19},{19,3},{4,20},{20... | collective-permute-start | bytes 172040 | tf_op jit(solution)/shard_map/ppermute | solution.py:371
  11.1 0.0 copy-done
  11.1 0.0 copy-done.1
  11.1 0.0 copy-done.2
  11.1 3.0 %shard_map.97 = (f32[96,1024]{1,0:T(8,128)S(1)}, bf16[4,24,640]{2,1,0:T(8,128)(2,1)S(1)}, bf16[96,1024]{1,0:T(8,128)(2,1)S(1)}, bf16[640,1024]{1,0:T(8,128)(2,1)S(1)}) custom-call(s32[1]{0:T(128)} %bitcast.row_ref, s32[1]{0:T(128)} %bitcast.3.parity_ref, s32[2]{0:T(128)S(1)} %copy-done.1, s32[2,2,8]{2,1,0:T(2,128)S(1)} %bitcast.5, s32[2,8]{1,0:T(2,128)S(1)} %copy-done, ...), custom_call_target="tpu_custom_call" | custom-call | flops 402653184 | bytes 3440848 | tf_op jit(solution)/shard_map/pallas_call | solution.py:327
  14.1 0.0 collective-permute-done.2.got_ref
  14.1 0.8 %shard_map.99 = (bf16[2,16,768]{2,1,0:T(8,128)(2,1)S(1)}, bf16[2,24,640]{2,1,0:T(8,128)(2,1)S(1)}, bf16[96,1024]{1,0:T(8,128)(2,1)S(1)}) custom-call(s32[1]{0:T(128)} %bitcast.row_ref, s32[2]{0:T(128)S(1)} %copy-done.1, s32[2,8]{1,0:T(2,128)S(1)} %copy-done, bf16[2,8,128,384]{3,2,1,0:T(8,128)(2,1)S(1)} %get-tuple-element.24.rest_0_.w_ref, ...), custom_call_target="tpu_custom_call" | custom-call | flops 201326592 | bytes 3334220 | tf_op jit(solution)/shard_map/pallas_call | solution.py:327
  14.9 1.2 %collective-permute-start.3 = (bf16[2,16,768]{2,1,0:T(8,128)(2,1)S(1)}, bf16[2,16,768]{2,1,0:T(8,128)(2,1)S(1)}, u32[]{:S(2)}, u32[]{:S(2)}) collective-permute-start(bf16[2,16,768]{2,1,0:T(8,128)(2,1)S(1)} %get-tuple-element.37), channel_id=1, source_target_pairs={{0,16},{16,0},{1,17},{17,1},{2,18},{18,2},{3,19},{19,3},{4,20},{20... | collective-permute-start | bytes 147464 | tf_op jit(solution)/shard_map/ppermute | solution.py:371
  16.1 2.1 %shard_map.100 = (f32[96,1024]{1,0:T(8,128)S(1)}, bf16[4,24,640]{2,1,0:T(8,128)(2,1)S(1)}, bf16[96,1024]{1,0:T(8,128)(2,1)S(1)}) custom-call(s32[1]{0:T(128)} %bitcast.row_ref, s32[1]{0:T(128)} %bitcast.3.parity_ref, s32[2]{0:T(128)S(1)} %copy-done.1, s32[2,2,8]{2,1,0:T(2,128)S(1)} %bitcast.6, s32[2,8]{1,0:T(2,128)S(1)} %copy-done, ...), custom_call_target="tpu_custom_call" | custom-call | flops 402653184 | bytes 3461328 | tf_op jit(solution)/shard_map/pallas_call | solution.py:327
  18.2 0.8 %collective-permute-done.3.got_ref = bf16[2,16,768]{2,1,0:T(8,128)(2,1)S(1)} collective-permute-done((bf16[2,16,768]{2,1,0:T(8,128)(2,1)S(1)}, bf16[2,16,768]{2,1,0:T(8,128)(2,1)S(1)}, u32[]{:S(2)}, u32[]{:S(2)}) %collective-permute-start.3) | collective-permute-done | bytes 49184 | tf_op jit(solution)/shard_map/ppermute | solution.py:371
  19.1 0.8 %shard_map.101 = (bf16[2,16,768]{2,1,0:T(8,128)(2,1)S(1)}, bf16[2,24,640]{2,1,0:T(8,128)(2,1)S(1)}, bf16[96,1024]{1,0:T(8,128)(2,1)S(1)}) custom-call(s32[1]{0:T(128)} %bitcast.row_ref, s32[2]{0:T(128)S(1)} %copy-done.1, s32[2,8]{1,0:T(2,128)S(1)} %copy-done, bf16[2,8,128,384]{3,2,1,0:T(8,128)(2,1)S(1)} %get-tuple-element.24.rest_0_.w_ref, ...), custom_call_target="tpu_custom_call" | custom-call | flops 201326592 | bytes 3326028 | tf_op jit(solution)/shard_map/pallas_call | solution.py:327
  19.9 1.2 %collective-permute-start.4 = (bf16[2,16,768]{2,1,0:T(8,128)(2,1)S(1)}, bf16[2,16,768]{2,1,0:T(8,128)(2,1)S(1)}, u32[]{:S(2)}, u32[]{:S(2)}) collective-permute-start(bf16[2,16,768]{2,1,0:T(8,128)(2,1)S(1)} %get-tuple-element.43), channel_id=1, source_target_pairs={{0,16},{16,0},{1,17},{17,1},{2,18},{18,2},{3,19},{19,3},{4,20},{20... | collective-permute-start | bytes 147464 | tf_op jit(solution)/shard_map/ppermute | solution.py:371
  21.1 2.8 %shard_map.102 = (f32[64,1024]{1,0:T(8,128)S(1)}, bf16[4,16,640]{2,1,0:T(8,128)(2,1)S(1)}, bf16[2,16,4,1024]{3,2,1,0:T(4,128)(2,1)}) custom-call(s32[1]{0:T(128)} %bitcast.row_ref, s32[1]{0:T(128)} %bitcast.3.parity_ref, s32[2]{0:T(128)S(1)} %copy-done.1, s32[2,2,8]{2,1,0:T(2,128)S(1)} %bitcast.7, s32[2,8]{1,0:T(2,128)S(1)} %copy-done, ...), custom_call_target="tpu_custom_call" | custom-call | flops 402653184 | bytes 3461328 | tf_op jit(solution)/shard_map/pallas_call | solution.py:327
  23.8 0.2 collective-permute-done.4.got_ref
  24.0 1.7 %shard_map.103 = (bf16[4,8,2560]{2,1,0:T(8,128)(2,1)}, bf16[2,16,4,1024]{3,2,1,0:T(4,128)(2,1)}) custom-call(s32[1]{0:T(128)} %bitcast.row_ref, s32[2]{0:T(128)S(1)} %copy-done.1, s32[2,8]{1,0:T(2,128)S(1)} %copy-done, bf16[2,8,128,384]{3,2,1,0:T(8,128)(2,1)S(1)} %get-tuple-element.24.rest_0_.w_ref, ...), custom_call_target="tpu_custom_call", output_to_operand_aliasing={{1}: (8, {})} | custom-call | flops 201326592 | bytes 3539020 | tf_op jit(solution)/shard_map/pallas_call | solution.py:327
  (1 shorter events, 0.0 us)
Async XLA Ops:
  0.6 10.4 %copy-start = (s32[2,8]{1,0:T(2,128)S(1)}, s32[2,8]{1,0:T(2,128)}, u32[]{:S(2)}) copy-start(s32[2,8]{1,0:T(2,128)} %iidx_ref.11) | copy-start | bytes 196
  0.7 10.4 %copy-start.1 = (s32[2]{0:T(128)S(1)}, s32[2]{0:T(128)}, u32[]{:S(2)}) copy-start(s32[2]{0:T(128)} %band_ref.11) | copy-start | bytes 28
  0.7 10.4 %copy-start.2 = (s32[2,8,2]{1,2,0:T(2,128)S(1)}, s32[2,8,2]{1,2,0:T(2,128)}, u32[]{:S(2)}) copy-start(s32[2,8,2]{1,2,0:T(2,128)} %param.11) | copy-start | bytes 388
  1.6 7.5 %collective-permute-start = (bf16[4,8,1024]{2,1,0:T(8,128)(2,1)S(1)}, bf16[4,8,1024]{2,1,0:T(8,128)(2,1)S(1)}, u32[]{:S(2)}, u32[]{:S(2)}) collective-permute-start(bf16[4,8,1024]{2,1,0:T(8,128)(2,1)S(1)} %get-tuple-element.28), channel_id=1, source_target_pairs={{0,15},{1,2},{2,1},{3,4},{4,3},{5,6},{6,5},{7,8},{8,7},{9,10},{10,... | collective-permute-start | bytes 196616 | tf_op jit(solution)/shard_map/ppermute | solution.py:367
  7.1 2.0 %collective-permute-start.1 = (bf16[4,8,1024]{2,1,0:T(8,128)(2,1)S(1)}, bf16[4,8,1024]{2,1,0:T(8,128)(2,1)S(1)}, u32[]{:S(2)}, u32[]{:S(2)}) collective-permute-start(bf16[4,8,1024]{2,1,0:T(8,128)(2,1)S(1)} %get-tuple-element.29), channel_id=1, source_target_pairs={{0,1},{1,0},{2,3},{3,2},{4,5},{5,4},{6,7},{7,6},{8,9},{9,8},{10,11... | collective-permute-start | bytes 196616 | tf_op jit(solution)/shard_map/ppermute | solution.py:367
  9.1 5.0 %collective-permute-start.2 = (bf16[2,16,896]{2,1,0:T(8,128)(2,1)S(1)}, bf16[2,16,896]{2,1,0:T(8,128)(2,1)S(1)}, u32[]{:S(2)}, u32[]{:S(2)}) collective-permute-start(bf16[2,16,896]{2,1,0:T(8,128)(2,1)S(1)} %shard_map.98), channel_id=1, source_target_pairs={{0,16},{16,0},{1,17},{17,1},{2,18},{18,2},{3,19},{19,3},{4,20},{20... | collective-permute-start | bytes 172040 | tf_op jit(solution)/shard_map/ppermute | solution.py:371
  14.9 4.2 %collective-permute-start.3 = (bf16[2,16,768]{2,1,0:T(8,128)(2,1)S(1)}, bf16[2,16,768]{2,1,0:T(8,128)(2,1)S(1)}, u32[]{:S(2)}, u32[]{:S(2)}) collective-permute-start(bf16[2,16,768]{2,1,0:T(8,128)(2,1)S(1)} %get-tuple-element.37), channel_id=1, source_target_pairs={{0,16},{16,0},{1,17},{17,1},{2,18},{18,2},{3,19},{19,3},{4,20},{20... | collective-permute-start | bytes 147464 | tf_op jit(solution)/shard_map/ppermute | solution.py:371
  19.9 4.2 %collective-permute-start.4 = (bf16[2,16,768]{2,1,0:T(8,128)(2,1)S(1)}, bf16[2,16,768]{2,1,0:T(8,128)(2,1)S(1)}, u32[]{:S(2)}, u32[]{:S(2)}) collective-permute-start(bf16[2,16,768]{2,1,0:T(8,128)(2,1)S(1)} %get-tuple-element.43), channel_id=1, source_target_pairs={{0,16},{16,0},{1,17},{17,1},{2,18},{18,2},{3,19},{19,3},{4,20},{20... | collective-permute-start | bytes 147464 | tf_op jit(solution)/shard_map/ppermute | solution.py:371

commit v4 on v3

v4 whole, which is shorter than its diff:
```python
import functools

import jax
import jax.numpy as jnp
from jax import lax
from jax.experimental import pallas as pl
from jax.experimental.pallas import tpu as pltpu
from jax.sharding import PartitionSpec as P

VARS = 40
STEPS = 3
CELL = 4 * VARS
CHUNK = 4 * CELL
HALF = 512
NEAR = 256
MEM = 4
BLK = 128
BF = jnp.bfloat16
F32 = jnp.float32
VM = pl.BlockSpec(memory_space=pltpu.VMEM)
SM = pl.BlockSpec(memory_space=pltpu.SMEM)
HB = pl.BlockSpec(memory_space=pltpu.HBM)
NT = (((1,), (1,)), ((), ()))


def row_of(slot, row_ref):
    return row_ref[0] if slot == 0 else 1 - row_ref[0]


def message_kernel(slots, row_ref, field_hbm, state_hbm, right_ref, left_ref, own_ref, *rest):
    field_ref, state_ref, sems = rest[3 * slots :]
    regions = state_hbm.shape[1]
    copies = [
        pltpu.make_async_copy(field_hbm, field_ref, sems.at[0]),
        pltpu.make_async_copy(state_hbm.at[:, pl.ds(regions - 2, 2)], state_ref.at[0], sems.at[1]),
        pltpu.make_async_copy(state_hbm.at[:, pl.ds(0, 2)], state_ref.at[1], sems.at[2]),
    ]
    for c in copies:
        c.start()
    for c in copies:
        c.wait()
    chunks = field_ref.shape[2] // CHUNK
    tiles = []
    for q in range(chunks):
        for m in range(MEM):
            tiles.append(field_ref[m, :, q * CHUNK : (q + 1) * CHUNK].astype(F32)[None])
    rows = jnp.transpose(jnp.concatenate(tiles, axis=0), (1, 0, 2)).astype(BF)
    own_ref[...] = rows
    last = (chunks - 1) * MEM
    for k, out in enumerate((right_ref, left_ref)):
        for r in range(2):
            for j in range(2):
                out[r, j * MEM : (j + 1) * MEM] = state_ref[k, r, j]
        for d in range(8):
            at, lane = (d % 2) * MEM, (d // 2 % 2) * HALF
            out[2 + d // 4, at : at + MEM, lane : lane + HALF] = rows[d, last:, CHUNK - HALF :] if k == 0 else rows[d, :MEM, :HALF]
    for slot in range(slots):
        low = row_of(slot, row_ref) == 0
        dright_ref, edge_ref, dleft_ref = rest[3 * slot : 3 * slot + 3]
        edge_ref[...] = jnp.zeros(edge_ref.shape, BF)
        dright_ref[...] = jnp.zeros(dright_ref.shape, BF)
        for k in range(2):
            row = jnp.where(low, rows[k], rows[6 + k])
            edge_ref[k, :, :CHUNK] = row
            dright_ref[0, k * MEM : (k + 1) * MEM, :HALF] = row[last:, CHUNK - HALF :]
            dleft_ref[k * MEM : (k + 1) * MEM] = row[:MEM, :HALF]


def own_kernel(row_ref, state_hbm, coup_hbm, inp_hbm, read_hbm, s0_ref, s1_ref, coup_ref, inp_ref, read_ref, state_ref, sems):
    pairs = [(state_hbm, state_ref), (coup_hbm, coup_ref), (inp_hbm, inp_ref), (read_hbm.at[0], read_ref)]
    copies = [pltpu.make_async_copy(src, dst, sems.at[i]) for i, (src, dst) in enumerate(pairs)]
    for c in copies:
        c.start()
    copies[0].wait()
    chunks = state_ref.shape[1] // 4
    for slot, s_ref in enumerate((s0_ref, s1_ref)):
        r = row_of(slot, row_ref)
        rows = [state_ref[r, 4 * q + res].astype(F32) for res in range(4) for q in range(chunks)]
        s_ref[...] = jnp.concatenate(rows, axis=0).astype(BF)
    for c in copies[1:]:
        c.wait()


def pack(row, out_ref, k):
    last = row.shape[0] - MEM
    out_ref[k, :, :CHUNK] = row[MEM:last].astype(BF)
    half = NEAR // 2
    ends = [row[:MEM, CHUNK - NEAR : CHUNK - half], row[:MEM, CHUNK - half :], row[last:, :half], row[last:, half:NEAR]]
    out_ref[k, :, CHUNK:] = jnp.concatenate(ends, axis=0).astype(BF)


def unpack(msg):
    x = msg.astype(F32)
    own, ends = x[:, :CHUNK], x[:, CHUNK:]
    fill = jnp.zeros((MEM, CHUNK - 2 * ends.shape[1]), F32)
    before = jnp.concatenate([fill, ends[:MEM], ends[MEM : 2 * MEM]], axis=1)
    after = jnp.concatenate([ends[2 * MEM : 3 * MEM], ends[3 * MEM :], fill], axis=1)
    return jnp.concatenate([before, own, after], axis=0)


def windows(lats, narrow):
    parts = [[] for _ in range(4)]
    for a in lats:
        rows = a.shape[0]
        before = jnp.concatenate([a[rows - MEM :, CHUNK - 2 * VARS :], a[: rows - MEM, CHUNK - 2 * VARS :]], axis=0)
        after = jnp.concatenate([a[MEM:, : 2 * VARS], a[:MEM, : 2 * VARS]], axis=0)
        ext = jnp.concatenate([before, a, after], axis=1)
        if narrow:
            ext = ext[MEM : rows - MEM]
        for res in range(4):
            parts[res].append(ext[:, CELL * res : CELL * res + 2 * CELL])
    return jnp.concatenate([jnp.concatenate(p, axis=1) for p in parts], axis=0).astype(BF)


def latitude(pred, d):
    per = pred.shape[0] // 4
    return jnp.concatenate([pred[res * per : (res + 1) * per, d * CELL : (d + 1) * CELL] for res in range(4)], axis=1)


def of_band(band, values, *at):
    got = values[(0, *at)]
    for g in range(1, values.shape[0]):
        got = jnp.where(band == g, values[(g, *at)], got)
    return got


def block_at(index, ref):
    return pl.multiple_of(jnp.clip(index, 0, ref.shape[1] // BLK - 1) * BLK, BLK)


def block_pre(b, band, s_ref, in_ref, cidx, iidx, coup_ref, inp_ref):
    pieces = []
    mats = [coup_ref[band, (2 * b + k) * BLK : (2 * b + k + 1) * BLK, :] for k in range(2)]
    mats.append(inp_ref[band, b * BLK : (b + 1) * BLK, :])
    for k in range(2):
        pieces.append(s_ref[:, pl.ds(block_at(of_band(band, cidx, k, b), s_ref), BLK)])
    pieces.append(in_ref[:, pl.ds(block_at(of_band(band, iidx, b), in_ref), BLK)])
    return lax.dot_general(jnp.concatenate(pieces, axis=1), jnp.concatenate(mats, axis=1), NT, preferred_element_type=F32)


def half_of(r, rest_lats):
    return pl.ds(pl.multiple_of((1 - r if rest_lats else r) * 2 * CELL, 2 * CELL), 2 * CELL)


def send_edge(r, state, read_ref, msg_ref, edge_ref, s_ref):
    s_ref[...] = state
    pred = lax.dot_general(state, read_ref[half_of(r, False), :], NT, preferred_element_type=F32)
    for d in range(2):
        row = latitude(pred, d)
        pack(row, msg_ref, d)
        edge_ref[d] = row.astype(BF)


def first_kernel(slot, edge, row_ref, band_ref, cidx_ref, iidx_ref, coup_ref, inp_ref, read_ref, own_ref, s0_ref, fl_ref, *rest):
    rest = list(rest)
    r = row_of(slot, row_ref)
    if edge:
        dl_ref, lat_ref, fr_ref, dr_ref = rest[:4]
        del rest[:4]
    else:
        fr_ref = rest.pop(0)
    outs, (xs_ref, s_ref, in_ref) = rest[:-3], rest[-3:]
    fill = jnp.zeros((MEM, CHUNK - HALF), F32)

    def widen(own, left, right):
        left = jnp.concatenate([fill, left.astype(F32)], axis=1)
        right = jnp.concatenate([right.astype(F32), fill], axis=1)
        return jnp.concatenate([left, own.astype(F32), right], axis=0)

    for d in range(8):
        at, lane = (d % 2) * MEM, (d // 2 % 2) * HALF
        left = fl_ref[2 + d // 4, at : at + MEM, lane : lane + HALF]
        right = fr_ref[2 + d // 4, at : at + MEM, lane : lane + HALF]
        xs_ref[2 + d] = widen(own_ref[d], left, right)
    for k in range(2):
        at = k * MEM
        if edge:
            xs_ref[10 * r + k] = widen(lat_ref[k, :, :CHUNK], dl_ref[0, at : at + MEM, :HALF], dr_ref[at : at + MEM])
        else:
            xs_ref[10 * r + k] = jnp.zeros(xs_ref.shape[1:], F32)
    empty = jnp.zeros((MEM, s0_ref.shape[1]), F32)
    per = s0_ref.shape[0] // 4
    rows = []
    for res in range(4):
        rows.append(fl_ref[r, (res - 2) * MEM : (res - 1) * MEM].astype(F32) if res >= 2 else empty)
        rows.append(s0_ref[res * per : (res + 1) * per].astype(F32))
        rows.append(fr_ref[r, res * MEM : (res + 1) * MEM].astype(F32) if res < 2 else empty)
    s_ref[...] = jnp.concatenate(rows, axis=0).astype(BF)
    in_ref[...] = windows([xs_ref[4 * r + d] for d in range(8)], False)
    bands, cidx, iidx = band_ref[...], cidx_ref[...], iidx_ref[...]
    band = jnp.where(r == 0, bands[0], bands[1])
    pres = [block_pre(b, band, s_ref, in_ref, cidx, iidx, coup_ref, inp_ref) for b in range(iidx_ref.shape[1])]
    state = jnp.concatenate([jnp.tanh(p).astype(BF) for p in pres], axis=1)
    if edge:
        send_edge(r, state, read_ref, *outs)
        return
    outs[1][...] = state
    pred = lax.dot_general(state, read_ref[...], NT, preferred_element_type=F32)
    for d in range(4):
        outs[0][d] = latitude(pred, d).astype(BF)


def narrowed(s):
    per = s.shape[0] // 4
    return jnp.concatenate([s[res * per + MEM : (res + 1) * per - MEM] for res in range(4)], axis=0)


def shadow_kernel(last, slots, row_ref, band_ref, cidx_ref, iidx_ref, coup_ref, inp_ref, read_ref, *rest):
    rest = list(rest)

    def take(n):
        got = rest[:n]
        del rest[:n]
        return got

    edge_refs, s_refs = take(slots), take(slots)
    far_refs = take(2 * (2 - slots))
    pre_refs = take(slots)
    out_far = take(2 * (2 - slots))
    xs_ref, in_ref = take(2)
    rows_at = [row_of(0, row_ref), row_of(1, row_ref)]
    for k in range(2):
        xs_ref[k] = jnp.zeros(xs_ref.shape[1:], F32)
        xs_ref[10 + k] = jnp.zeros(xs_ref.shape[1:], F32)
    for slot in range(slots):
        r = rows_at[slot]
        pred = lax.dot_general(s_refs[slot][...], read_ref[half_of(r, True), :], NT, preferred_element_type=F32)
        for d in range(2):
            xs_ref[2 + 4 * r + 2 * r + d] = edge_refs[slot][d].astype(F32)
            xs_ref[2 + 4 * r + 2 * (1 - r) + d] = latitude(pred, d).astype(BF).astype(F32)
    if far_refs:
        for d in range(4):
            xs_ref[2 + 4 * rows_at[1] + d] = far_refs[0][d].astype(F32)
        s_refs = [s_refs[0], far_refs[1]]
    if last:
        short_refs = take(2)
        for slot in range(2):
            short_refs[slot][...] = narrowed(s_refs[slot][...].astype(F32)).astype(BF)
        s_refs = short_refs

    bands, cidx, iidx = band_ref[...], cidx_ref[...], iidx_ref[...]
    copy = None
    for slot in (1, 0):
        r = rows_at[slot]
        band = jnp.where(r == 0, bands[0], bands[1])
        in_ref[...] = windows([xs_ref[4 * r + d] for d in range(8)], last)
        blocks = iidx_ref.shape[1]
        pres = [block_pre(b, band, s_refs[slot], in_ref, cidx, iidx, coup_ref, inp_ref) for b in range(blocks)]
        if slot < slots:
            for b in range(blocks):
                pre_refs[slot][:, b * BLK : (b + 1) * BLK] = pres[b]
            continue
        state = jnp.concatenate([jnp.tanh(p).astype(BF) for p in pres], axis=1)
        if last:
            stage_ref, sem = take(2)
            copy = put_states(r, state, stage_ref, out_far[1], sem)
        else:
            out_far[1][...] = state
        pred = lax.dot_general(state, read_ref[...], NT, preferred_element_type=F32)
        for d in range(4):
            out_far[0][d] = latitude(pred, d).astype(BF)
    if copy is not None:
        copy.wait()


def put_states(r, state, stage_ref, states_hbm, sem):
    per = state.shape[0] // 4
    for res in range(4):
        for q in range(per // MEM):
            at = res * per + q * MEM
            stage_ref[4 * q + res] = state[at : at + MEM]
    copy = pltpu.make_async_copy(stage_ref, states_hbm.at[r], sem)
    copy.start()
    return copy


def late_kernel(slot, last, final, row_ref, band_ref, iidx_ref, inp_ref, read_ref, pre_ref, got_ref, *rest):
    r = row_of(slot, row_ref)
    bands, iidx = band_ref[...], iidx_ref[...]
    band = jnp.where(r == 0, bands[0], bands[1])
    in_ref = rest[-1]
    in_ref[...] = windows([unpack(got_ref[k]) for k in range(2)], last)
    parts = []
    for b in range(iidx_ref.shape[1]):
        k = of_band(band, iidx, b) - 15 * r
        used = jnp.logical_and(k >= 0, k < 5)
        at = pl.multiple_of(jnp.where(used, k, 0) * BLK, BLK)
        term = lax.dot_general(in_ref[:, pl.ds(at, BLK)], inp_ref[band, b * BLK : (b + 1) * BLK, :], NT, preferred_element_type=F32)
        pre = pre_ref[:, b * BLK : (b + 1) * BLK] + jnp.where(used, term, 0.0)
        parts.append(jnp.tanh(pre).astype(BF))
    state = jnp.concatenate(parts, axis=1)
    if not last:
        send_edge(r, state, read_ref, *rest[:3])
        return
    if not final:
        lats_ref, states_hbm, stage_ref, sem = rest[:4]
    else:
        other_ref, _, field_hbm, states_hbm, stage_ref, sem, field_ref, field_sem = rest[:8]
    copy = put_states(r, state, stage_ref, states_hbm, sem)
    pred = lax.dot_general(state, read_ref[...], NT, preferred_element_type=F32)
    mine = [latitude(pred, d) for d in range(4)]
    if not final:
        for d in range(4):
            lats_ref[d] = mine[d].astype(BF)
        copy.wait()
        return
    other = [other_ref[d].astype(F32) for d in range(4)]
    low = r == 0
    rows = [jnp.where(low, mine[d], other[d])[None] for d in range(4)]
    rows += [jnp.where(low, other[d], mine[d])[None] for d in range(4)]
    tiles = jnp.transpose(jnp.concatenate(rows, axis=0), (1, 0, 2)).astype(BF)
    for q in range(field_ref.shape[2] // CHUNK):
        for m in range(MEM):
            field_ref[m, :, q * CHUNK : (q + 1) * CHUNK] = tiles[q * MEM + m]
    out = pltpu.make_async_copy(field_ref, field_hbm, field_sem)
    out.start()
    copy.wait()
    out.wait()


def call(kernel, out_shape, out_specs, scratch, operands, flops=0, aliases=None):
    arrays = [pltpu.with_memory_space_constraint(x, pltpu.HBM) if s is HB else x for x, s in operands]
    size = sum(x.size * x.dtype.itemsize for x, _ in operands)
    return pl.pallas_call(
        kernel,
        out_shape=out_shape,
        in_specs=[s for _, s in operands],
        out_specs=out_specs,
        scratch_shapes=scratch,
        input_output_aliases=aliases or {},
        compiler_params=pltpu.CompilerParams(vmem_limit_bytes=40 * 1024 * 1024),
        cost_estimate=pl.CostEstimate(flops=flops, bytes_accessed=size, transcendentals=0),
    )(*arrays)


def per_device(field_state, reservoir_state, coupling_blocks, coupling_index, input_blocks, input_index, readout, region_band):
    lat_count, lon_count = lax.axis_size("lat"), lax.axis_size("lon")
    lat_at = lax.axis_index("lat").astype(jnp.int32)
    region_rows, regions, members, units = reservoir_state.shape
    outs = readout.shape[1]
    assert region_rows == 2 and members == MEM and regions % 4 == 0
    chunks = regions // 4
    own_rows = chunks * MEM
    wide = own_rows + 2 * MEM
    rows = 4 * wide
    short = 4 * own_rows
    swap = lat_count == 2
    slots = 1 if swap else 2

    def bf(*dims):
        return jax.ShapeDtypeStruct(dims, BF)

    def vm(dims, dtype=BF):
        return pltpu.VMEM(dims, dtype)

    def send(x, lat_step, lon_step):
        pairs = []
        for i in range(lat_count):
            to = 1 - i if swap and lat_step else i + lat_step
            if 0 <= to < lat_count:
                for j in range(lon_count):
                    pairs.append((i * lon_count + j, to * lon_count + (j + lon_step) % lon_count))
        return lax.ppermute(x, ("lat", "lon"), pairs)

    def across(xs, lon_step=0):
        if swap:
            return [send(xs[0], 1, lon_step)]
        return [send(xs[1], 1, lon_step), send(xs[0], -1, lon_step)]

    row = ((1 - lat_at if swap else lat_at * 0).reshape(1), SM)
    small = [(region_band, VM), (coupling_index.transpose(0, 2, 1), VM), (input_index, VM)]
    band, _, iidx = small
    flops = 2 * rows * units * (3 * BLK + outs)

    mail = call(
        functools.partial(message_kernel, slots),
        [bf(4, 2 * MEM, 2 * HALF)] * 2 + [bf(8, own_rows, CHUNK)] + [bf(4, 2 * MEM, 2 * HALF), bf(2, own_rows, 4 * HALF * 2 * MEM // own_rows), bf(2 * MEM, HALF)] * slots,
        [VM] * (3 + 3 * slots),
        [vm(field_state.shape), vm((2, region_rows, 2, MEM, units)), pltpu.SemaphoreType.DMA((3,))],
        [row, (field_state, HB), (reservoir_state, HB)],
    )
    from_left = send(mail[0], 0, 1)
    from_dleft = across(mail[3::3], 1)
    from_lat = across(mail[4::3])
    from_right = send(mail[1], 0, -1)
    from_dright = across(mail[5::3], -1)
    own = (mail[2], VM)
    s0, s1, coup, inp, read = call(
        own_kernel,
        [bf(short, units), bf(short, units), bf(*coupling_blocks.shape), bf(*input_blocks.shape), bf(outs, units)],
        [VM] * 5,
        [vm(reservoir_state.shape), pltpu.SemaphoreType.DMA((4,))],
        [row, (reservoir_state, HB), (coupling_blocks, HB), (input_blocks, HB), (readout, HB)],
        flops,
    )
    weights = [(x, VM) for x in (coup, inp, read)]
    states_shape = bf(region_rows, regions, MEM, units)
    stage = [vm((regions, MEM, units)), pltpu.SemaphoreType.DMA]
    padded = vm((12, wide, CHUNK), F32)
    send_out = [bf(2, own_rows, CHUNK + NEAR // 2), bf(2, wide, CHUNK), bf(rows, units)]

    sent, edges, states, far = [None] * slots, [None] * slots, [None] * slots, []
    for slot in range(2):
        edge = slot < slots
        operands = [row] + small + weights + [own, ((s0, s1)[slot], VM), (from_left, VM)]
        if edge:
            operands += [(from_dleft[slot], VM), (from_lat[slot], VM)]
        operands.append((from_right, VM))
        if edge:
            operands.append((from_dright[slot], VM))
        got = call(
            functools.partial(first_kernel, slot, edge),
            send_out if edge else [bf(4, wide, CHUNK), bf(rows, units)],
            [VM] * (3 if edge else 2),
            [padded, vm((rows, units)), vm((rows, 16 * CELL))],
            operands,
            flops,
        )
        if edge:
            sent[slot], edges[slot], states[slot] = got
        else:
            far = list(got)

    for step in range(1, STEPS):
        last = step == STEPS - 1
        got = across(sent)
        pre_rows = short if last else rows
        out = [jax.ShapeDtypeStruct((pre_rows, units), F32)] * slots
        specs = [VM] * slots
        scratch = [padded, vm((pre_rows, 16 * CELL))] + [vm((short, units))] * (2 if last else 0)
        if swap:
            out += [bf(4, own_rows if last else wide, CHUNK), states_shape if last else bf(rows, units)]
            specs += [VM, HB if last else VM]
            scratch += stage if last else []
        shadow = call(
            functools.partial(shadow_kernel, last, slots),
            out,
            specs,
            scratch,
            [row] + small + weights + [(x, VM) for x in edges + states + far],
            2 * flops,
        )
        far = list(shadow[slots:])
        for slot in reversed(range(slots)):
            operands = [row, band, iidx] + weights[1:] + [(shadow[slot], VM), (got[slot], VM)]
            inputs = [vm((pre_rows, 4 * CELL))]
            if not last:
                sent[slot], edges[slot], states[slot] = call(
                    functools.partial(late_kernel, slot, False, False), send_out, [VM] * 3, inputs, operands, flops
                )
            elif slot == 1:
                far = call(
                    functools.partial(late_kernel, slot, True, False),
                    [bf(4, own_rows, CHUNK), states_shape],
                    [VM, HB],
                    stage + inputs,
                    operands,
                    flops,
                )
            else:
                return call(
                    functools.partial(late_kernel, slot, True, True),
                    [bf(MEM, 8, regions * CELL), states_shape],
                    [HB, HB],
                    stage + [vm((MEM, 8, regions * CELL)), pltpu.SemaphoreType.DMA] + inputs,
                    operands + [(far[0], VM), (far[1], HB)],
                    flops,
                    {len(operands) + 1: 1},
                )


def solution(mesh):
    return jax.shard_map(
        per_device,
        mesh=mesh,
        in_specs=(
            P(None, "lat", "lon"),
            P("lat", "lon", None, None),
            P("lat", None, None),
            P("lat", None, None),
            P("lat", None, None),
            P("lat", None),
            P("lat", None, None),
            P("lat"),
        ),
        out_specs=(P(None, "lat", "lon"), P("lat", "lon", None, None)),
        check_vma=False,
    )
```

time: 26 us -> 24.9 us (0.958)
  starting transfers between devices: 9.89 us -> 11.2 us
  Pallas kernels: 13.7 us -> 12.5 us
  waiting for transfers between devices: 1.4 us -> 0.34 us
    ppermute x5 -> x7, starting transfers between devices: 9.89 us -> 11.2 us  [send(): return lax.ppermute(x, ('lat', 'lon'), pairs)]
    pallas_call x9 -> x8, Pallas kernels: 13.7 us -> 12.5 us  [call(): pl.pallas_call(kernel, out_shape=out_shape, in_specs=[s for _, s in opera...]
    ppermute x5 -> x7, waiting for transfers between devices: 1.4 us -> 0.34 us  [send(): return lax.ppermute(x, ('lat', 'lon'), pairs)]
  transfers between devices with their start and end apart: 5 -> 7, of which waited for: 3 -> 1; matrix products, arithmetic and copies ran while one was open for 0% -> 0% of each run, Pallas kernels for 37% -> 32%
where the time goes in v4:
time: 24.9 us; the launch traced here: 24.8 us
  Pallas kernels  12.5 us (50%)
  starting transfers between devices  11.2 us (45%)
  between operations  0.77 us (3%)
  waiting for transfers between devices  0.34 us (1%)
    pallas_call x8, Pallas kernels, call(): pl.pallas_call(kernel, out_shape=out_shape, in_specs=[s for _, s in opera...  12.5 us
    ppermute x7, starting transfers between devices, send(): return lax.ppermute(x, ('lat', 'lon'), pairs)  11.2 us
  transfers between devices with their start and end apart: 7, of which 1 were waited for; matrix products, arithmetic and copies ran while one was open for 0% of the time, Pallas kernels for 32%

profile of v4, /device:TPU:0, one launch (start us, length us, event | category | flops | bytes accessed | tf_op | source)
XLA Modules:
  0.0 24.8 jit_solution(6862884174267281030)
XLA Ops:
  0.6 1.1 %shard_map.96 = (bf16[4,8,1024]{2,1,0:T(8,128)(2,1)S(1)}, bf16[4,8,1024]{2,1,0:T(8,128)(2,1)S(1)}, bf16[8,16,640]{2,1,0:T(8,128)(2,1)S(1)}, bf16[4,8,1024]{2,1,0...) custom-call(s32[1]{0:T(128)} %bitcast.row_ref, bf16[4,8,2560]{2,1,0:T(8,128)(2,1)} %field_hbm.1, ...), custom_call_target="tpu_custom_call" | custom-call | bytes 425988 | tf_op jit(solution)/shard_map/pallas_call | solution.py:324
  1.7 0.5 %collective-permute-start = (bf16[4,8,1024]{2,1,0:T(8,128)(2,1)S(1)}, bf16[4,8,1024]{2,1,0:T(8,128)(2,1)S(1)}, u32[]{:S(2)}, u32[]{:S(2)}) collective-permute-start(bf16[4,8,1024]{2,1,0:T(8,128)(2,1)S(1)} %get-tuple-element.32), channel_id=1, source_target_pairs={{0,1},{1,2},{2,3},{3,4},{4,5},{5,6},{6,7},{7,8},{8,9},{9,10},{10,1... | collective-permute-start | bytes 196616 | tf_op jit(solution)/shard_map/ppermute | solution.py:363
  2.2 3.7 %collective-permute-start.1 = (bf16[4,8,1024]{2,1,0:T(8,128)(2,1)S(1)}, bf16[4,8,1024]{2,1,0:T(8,128)(2,1)S(1)}, u32[]{:S(2)}, u32[]{:S(2)}) collective-permute-start(bf16[4,8,1024]{2,1,0:T(8,128)(2,1)S(1)} %get-tuple-element.33), channel_id=1, source_target_pairs={{0,17},{1,18},{2,19},{3,20},{4,21},{5,22},{6,23},{7,24},{8,25},{9,... | collective-permute-start | bytes 196616 | tf_op jit(solution)/shard_map/ppermute | solution.py:363
  5.9 0.5 %collective-permute-start.2 = (bf16[2,16,1024]{2,1,0:T(8,128)(2,1)S(1)}, bf16[2,16,1024]{2,1,0:T(8,128)(2,1)S(1)}, u32[]{:S(2)}, u32[]{:S(2)}) collective-permute-start(bf16[2,16,1024]{2,1,0:T(8,128)(2,1)S(1)} %get-tuple-element.34), channel_id=1, source_target_pairs={{0,16},{1,17},{2,18},{3,19},{4,20},{5,21},{6,22},{7,23},{8,24},{9,... | collective-permute-start | bytes 196616 | tf_op jit(solution)/shard_map/ppermute | solution.py:363
  6.5 2.4 %collective-permute-start.3 = (bf16[4,8,1024]{2,1,0:T(8,128)(2,1)S(1)}, bf16[4,8,1024]{2,1,0:T(8,128)(2,1)S(1)}, u32[]{:S(2)}, u32[]{:S(2)}) collective-permute-start(bf16[4,8,1024]{2,1,0:T(8,128)(2,1)S(1)} %get-tuple-element.35), channel_id=1, source_target_pairs={{0,15},{1,0},{2,1},{3,2},{4,3},{5,4},{6,5},{7,6},{8,7},{9,8},{10,9... | collective-permute-start | bytes 196616 | tf_op jit(solution)/shard_map/ppermute | solution.py:363
  8.9 0.0 copy-start
  8.9 0.0 copy-start.1
  8.9 0.0 copy-start.2
  8.9 1.8 %collective-permute-start.4 = (bf16[8,512]{1,0:T(8,128)(2,1)S(1)}, bf16[8,512]{1,0:T(8,128)(2,1)S(1)}, u32[]{:S(2)}, u32[]{:S(2)}) collective-permute-start(bf16[8,512]{1,0:T(8,128)(2,1)S(1)} %get-tuple-element.36), channel_id=1, source_target_pairs={{0,31},{1,16},{2,17},{3,18},{4,19},{5,20},{6,21},{7,22},{8,23},{9,... | collective-permute-start | bytes 24584 | tf_op jit(solution)/shard_map/ppermute | solution.py:363
  10.7 1.9 %shard_map.95 = (bf16[64,1024]{1,0:T(8,128)(2,1)S(1)}, bf16[64,1024]{1,0:T(8,128)(2,1)S(1)}, bf16[2,2048,128]{2,1,0:T(8,128)(2,1)S(1)}, bf16[2,1024,128]{2,1,0:T(8,128)(2,1)S(1)}, bf16[640,1024]{1,0:T(8,128)(2,1)S(1)}) custom-call(s32[1]{0:T(128)} %bitcast.row_ref, bf16[2,16,4,1024]{3,2,1,0:T(4,128)(2,1)} %state_hbm.3, bf16[2,2048,128]{2,1,0:T(8,128)(2,1)} %coup_hbm.1, ...), custom_call_target="tpu_custom_call" | custom-call | flops 201326592 | bytes 3145732 | tf_op jit(solution)/shard_map/pallas_call | solution.py:324
  12.6 0.0 collective-permute-done.4.rest_3_
  12.7 0.0 collective-permute-done.fl_ref
  12.7 0.0 collective-permute-done.1.rest_0_
  12.7 0.0 collective-permute-done.2.rest_1_
  12.7 0.0 collective-permute-done.3.rest_2_.rest_0_
  12.7 0.0 copy-done
  12.7 0.0 copy-done.1
  12.7 0.0 copy-done.2
  12.7 1.1 %shard_map.97 = (bf16[2,16,768]{2,1,0:T(8,128)(2,1)S(1)}, bf16[2,24,640]{2,1,0:T(8,128)(2,1)S(1)}, bf16[96,1024]{1,0:T(8,128)(2,1)S(1)}) custom-call(s32[1]{0:T(128)} %bitcast.row_ref, s32[2]{0:T(128)S(1)} %copy-done.2, s32[2,2,8]{2,1,0:T(2,128)S(1)} %bitcast.2, s32[2,8]{1,0:T(2,128)S(1)} %copy-done, bf16[2,2048,128]{2,1,0:T(8,128)(2,1)S(1)} %get-tuple-element.29.coup_ref, ...), custom_call_target="tpu_custom_call" | custom-call | flops 201326592 | bytes 3449036 | tf_op jit(solution)/shard_map/pallas_call | solution.py:324
  13.9 0.9 %collective-permute-start.5 = (bf16[2,16,768]{2,1,0:T(8,128)(2,1)S(1)}, bf16[2,16,768]{2,1,0:T(8,128)(2,1)S(1)}, u32[]{:S(2)}, u32[]{:S(2)}) collective-permute-start(bf16[2,16,768]{2,1,0:T(8,128)(2,1)S(1)} %get-tuple-element.43), channel_id=1, source_target_pairs={{0,16},{1,17},{2,18},{3,19},{4,20},{5,21},{6,22},{7,23},{8,24},{9,... | collective-permute-start | bytes 147464 | tf_op jit(solution)/shard_map/ppermute | solution.py:363
  14.7 1.3 %shard_map.98 = (bf16[4,24,640]{2,1,0:T(8,128)(2,1)S(1)}, bf16[96,1024]{1,0:T(8,128)(2,1)S(1)}) custom-call(s32[1]{0:T(128)} %bitcast.row_ref, s32[2]{0:T(128)S(1)} %copy-done.2, s32[2,2,8]{2,1,0:T(2,128)S(1)} %bitcast.3, s32[2,8]{1,0:T(2,128)S(1)} %copy-done, bf16[2,2048,128]{2,1,0:T(8,128)(2,1)S(1)} %get-tuple-element.29.coup_ref, ...), custom_call_target="tpu_custom_call" | custom-call | flops 201326592 | bytes 3309772 | tf_op jit(solution)/shard_map/pallas_call | solution.py:324
  16.1 2.1 %shard_map.99 = (f32[96,1024]{1,0:T(8,128)S(1)}, bf16[4,24,640]{2,1,0:T(8,128)(2,1)S(1)}, bf16[96,1024]{1,0:T(8,128)(2,1)S(1)}) custom-call(s32[1]{0:T(128)} %bitcast.row_ref, s32[2]{0:T(128)S(1)} %copy-done.2, s32[2,2,8]{2,1,0:T(2,128)S(1)} %bitcast.4, s32[2,8]{1,0:T(2,128)S(1)} %copy-done, bf16[2,2048,128]{2,1,0:T(8,128)(2,1)S(1)} %get-tuple-element.29.coup_ref, ...), custom_call_target="tpu_custom_call" | custom-call | flops 402653184 | bytes 3461324 | tf_op jit(solution)/shard_map/pallas_call | solution.py:324
  18.1 0.0 collective-permute-done.5.got_ref
  18.1 0.8 %shard_map.100 = (bf16[2,16,768]{2,1,0:T(8,128)(2,1)S(1)}, bf16[2,24,640]{2,1,0:T(8,128)(2,1)S(1)}, bf16[96,1024]{1,0:T(8,128)(2,1)S(1)}) custom-call(s32[1]{0:T(128)} %bitcast.row_ref, s32[2]{0:T(128)S(1)} %copy-done.2, s32[2,8]{1,0:T(2,128)S(1)} %copy-done, bf16[2,1024,128]{2,1,0:T(8,128)(2,1)S(1)} %get-tuple-element.27.inp_ref, ...), custom_call_target="tpu_custom_call" | custom-call | flops 201326592 | bytes 2277452 | tf_op jit(solution)/shard_map/pallas_call | solution.py:324
  18.9 1.3 %collective-permute-start.6 = (bf16[2,16,768]{2,1,0:T(8,128)(2,1)S(1)}, bf16[2,16,768]{2,1,0:T(8,128)(2,1)S(1)}, u32[]{:S(2)}, u32[]{:S(2)}) collective-permute-start(bf16[2,16,768]{2,1,0:T(8,128)(2,1)S(1)} %get-tuple-element.49), channel_id=1, source_target_pairs={{0,16},{1,17},{2,18},{3,19},{4,20},{5,21},{6,22},{7,23},{8,24},{9,... | collective-permute-start | bytes 147464 | tf_op jit(solution)/shard_map/ppermute | solution.py:363
  20.2 2.5 %shard_map.101 = (f32[64,1024]{1,0:T(8,128)S(1)}, bf16[4,16,640]{2,1,0:T(8,128)(2,1)S(1)}, bf16[2,16,4,1024]{3,2,1,0:T(4,128)(2,1)}) custom-call(s32[1]{0:T(128)} %bitcast.row_ref, s32[2]{0:T(128)S(1)} %copy-done.2, s32[2,2,8]{2,1,0:T(2,128)S(1)} %bitcast.5, s32[2,8]{1,0:T(2,128)S(1)} %copy-done, bf16[2,2048,128]{2,1,0:T(8,128)(2,1)S(1)} %get-tuple-element.29.coup_ref, ...), custom_call_target="tpu_custom_call" | custom-call | flops 402653184 | bytes 3461324 | tf_op jit(solution)/shard_map/pallas_call | solution.py:324
  22.8 0.3 %collective-permute-done.6.got_ref = bf16[2,16,768]{2,1,0:T(8,128)(2,1)S(1)} collective-permute-done((bf16[2,16,768]{2,1,0:T(8,128)(2,1)S(1)}, bf16[2,16,768]{2,1,0:T(8,128)(2,1)S(1)}, u32[]{:S(2)}, u32[]{:S(2)}) %collective-permute-start.6) | collective-permute-done | bytes 49184 | tf_op jit(solution)/shard_map/ppermute | solution.py:363
  23.1 1.7 %shard_map.102 = (bf16[4,8,2560]{2,1,0:T(8,128)(2,1)}, bf16[2,16,4,1024]{3,2,1,0:T(4,128)(2,1)}) custom-call(s32[1]{0:T(128)} %bitcast.row_ref, s32[2]{0:T(128)S(1)} %copy-done.2, s32[2,8]{1,0:T(2,128)S(1)} %copy-done, bf16[2,1024,128]{2,1,0:T(8,128)(2,1)S(1)} %get-tuple-element.27.inp_ref, ...), custom_call_target="tpu_custom_call", output_to_operand_aliasing={{1}: (8, {})} | custom-call | flops 201326592 | bytes 2490444 | tf_op jit(solution)/shard_map/pallas_call | solution.py:324
Async XLA Ops:
  1.7 11.0 %collective-permute-start = (bf16[4,8,1024]{2,1,0:T(8,128)(2,1)S(1)}, bf16[4,8,1024]{2,1,0:T(8,128)(2,1)S(1)}, u32[]{:S(2)}, u32[]{:S(2)}) collective-permute-start(bf16[4,8,1024]{2,1,0:T(8,128)(2,1)S(1)} %get-tuple-element.32), channel_id=1, source_target_pairs={{0,1},{1,2},{2,3},{3,4},{4,5},{5,6},{6,7},{7,8},{8,9},{9,10},{10,1... | collective-permute-start | bytes 196616 | tf_op jit(solution)/shard_map/ppermute | solution.py:363
  2.2 10.5 %collective-permute-start.1 = (bf16[4,8,1024]{2,1,0:T(8,128)(2,1)S(1)}, bf16[4,8,1024]{2,1,0:T(8,128)(2,1)S(1)}, u32[]{:S(2)}, u32[]{:S(2)}) collective-permute-start(bf16[4,8,1024]{2,1,0:T(8,128)(2,1)S(1)} %get-tuple-element.33), channel_id=1, source_target_pairs={{0,17},{1,18},{2,19},{3,20},{4,21},{5,22},{6,23},{7,24},{8,25},{9,... | collective-permute-start | bytes 196616 | tf_op jit(solution)/shard_map/ppermute | solution.py:363
  5.9 6.7 %collective-permute-start.2 = (bf16[2,16,1024]{2,1,0:T(8,128)(2,1)S(1)}, bf16[2,16,1024]{2,1,0:T(8,128)(2,1)S(1)}, u32[]{:S(2)}, u32[]{:S(2)}) collective-permute-start(bf16[2,16,1024]{2,1,0:T(8,128)(2,1)S(1)} %get-tuple-element.34), channel_id=1, source_target_pairs={{0,16},{1,17},{2,18},{3,19},{4,20},{5,21},{6,22},{7,23},{8,24},{9,... | collective-permute-start | bytes 196616 | tf_op jit(solution)/shard_map/ppermute | solution.py:363
  6.5 6.2 %collective-permute-start.3 = (bf16[4,8,1024]{2,1,0:T(8,128)(2,1)S(1)}, bf16[4,8,1024]{2,1,0:T(8,128)(2,1)S(1)}, u32[]{:S(2)}, u32[]{:S(2)}) collective-permute-start(bf16[4,8,1024]{2,1,0:T(8,128)(2,1)S(1)} %get-tuple-element.35), channel_id=1, source_target_pairs={{0,15},{1,0},{2,1},{3,2},{4,3},{5,4},{6,5},{7,6},{8,7},{9,8},{10,9... | collective-permute-start | bytes 196616 | tf_op jit(solution)/shard_map/ppermute | solution.py:363
  8.9 3.8 %copy-start = (s32[2,8]{1,0:T(2,128)S(1)}, s32[2,8]{1,0:T(2,128)}, u32[]{:S(2)}) copy-start(s32[2,8]{1,0:T(2,128)} %iidx_ref.11) | copy-start | bytes 196
  8.9 3.8 %copy-start.1 = (s32[2,8,2]{1,2,0:T(2,128)S(1)}, s32[2,8,2]{1,2,0:T(2,128)}, u32[]{:S(2)}) copy-start(s32[2,8,2]{1,2,0:T(2,128)} %param.11) | copy-start | bytes 388
  8.9 3.8 %copy-start.2 = (s32[2]{0:T(128)S(1)}, s32[2]{0:T(128)}, u32[]{:S(2)}) copy-start(s32[2]{0:T(128)} %band_ref.11) | copy-start | bytes 28
  8.9 3.7 %collective-permute-start.4 = (bf16[8,512]{1,0:T(8,128)(2,1)S(1)}, bf16[8,512]{1,0:T(8,128)(2,1)S(1)}, u32[]{:S(2)}, u32[]{:S(2)}) collective-permute-start(bf16[8,512]{1,0:T(8,128)(2,1)S(1)} %get-tuple-element.36), channel_id=1, source_target_pairs={{0,31},{1,16},{2,17},{3,18},{4,19},{5,20},{6,21},{7,22},{8,23},{9,... | collective-permute-start | bytes 24584 | tf_op jit(solution)/shard_map/ppermute | solution.py:363
  13.9 4.3 %collective-permute-start.5 = (bf16[2,16,768]{2,1,0:T(8,128)(2,1)S(1)}, bf16[2,16,768]{2,1,0:T(8,128)(2,1)S(1)}, u32[]{:S(2)}, u32[]{:S(2)}) collective-permute-start(bf16[2,16,768]{2,1,0:T(8,128)(2,1)S(1)} %get-tuple-element.43), channel_id=1, source_target_pairs={{0,16},{1,17},{2,18},{3,19},{4,20},{5,21},{6,22},{7,23},{8,24},{9,... | collective-permute-start | bytes 147464 | tf_op jit(solution)/shard_map/ppermute | solution.py:363
  18.9 4.2 %collective-permute-start.6 = (bf16[2,16,768]{2,1,0:T(8,128)(2,1)S(1)}, bf16[2,16,768]{2,1,0:T(8,128)(2,1)S(1)}, u32[]{:S(2)}, u32[]{:S(2)}) collective-permute-start(bf16[2,16,768]{2,1,0:T(8,128)(2,1)S(1)} %get-tuple-element.49), channel_id=1, source_target_pairs={{0,16},{1,17},{2,18},{3,19},{4,20},{5,21},{6,22},{7,23},{8,24},{9,... | collective-permute-start | bytes 147464 | tf_op jit(solution)/shard_map/ppermute | solution.py:363
